TPU v7x, 128 devices: a whole 4x4x4 slice. The times are simulated.
128 devices in a mesh: wide: 32 (over y, z, core), narrow: 4 (over x).
Axes of the slice: x: 4, y: 4, z: 4, core: 2. Of those that a mesh axis runs over, the one named last changes fastest.
Arguments:
- traces: bfloat16 [32, 4, 64, 24, 512], P('wide', 'narrow'), may hold values from -6 to 6
- pair_first: int32 [32, 4, 9, 32], P('wide', 'narrow'), may hold values from 0 to 63
- pair_second: int32 [32, 4, 9, 32], P('wide', 'narrow'), may hold values from 0 to 63
- pair_valid: int32 [32, 4, 9, 32], P('wide', 'narrow'), may hold values from 0 to 1, as said below
Outputs:
- corr_sum: float32 [32, 4, 64, 24, 256], P('wide', 'narrow')
Inputs may be any that keep to these rules, and one draw needn't show every extreme that they name: `pair_valid`: 0 in every direction that points outside the grid of cells; slot 0 of every direction inside the grid is 1; cells differ in the share of live slots.
All inputs are finite; a program needn't handle non-finite values.
Results may differ from a plain program's by a relative error of at most 0.0003.
Values may be sent and summed in bfloat16 or wider, within the bound.
A program may use at most 256 MiB of HBM per device.

v0:
```python
import math

import jax
import jax.numpy as jnp
from jax import lax
from jax.sharding import PartitionSpec as P

LAGS = 256
NFFT = 640


def with_halo(cells, sides, width):
    for axis, dim in sides:
        count = lax.axis_size(axis)
        ends = count - 1
        head = lax.slice_in_dim(cells, 0, width, axis=dim)
        tail = lax.slice_in_dim(cells, cells.shape[dim] - width, cells.shape[dim], axis=dim)
        cells = jnp.concatenate(
            [
                lax.ppermute(tail, axis, [(i, (i + 1) % count) for i in range(ends)]),
                cells,
                lax.ppermute(head, axis, [((i + 1) % count, i) for i in range(ends)]),
            ],
            axis=dim,
        )
    return cells


def passed_along(x, axis, by):
    peers = lax.axis_size(axis)
    pairs = [(i, i + by) for i in range(peers) if 0 <= i + by < peers]
    return lax.ppermute(x, axis, pairs)


def make_tables(samples, nfft, lags):
    half_bins = nfft // 2
    half_lags = lags // 2
    angle_step = 2.0 * math.pi / nfft
    sample_ids = jnp.arange(samples, dtype=jnp.int32)
    bin_ids = jnp.arange(half_bins, dtype=jnp.int32)
    phase = (sample_ids[:, None] * bin_ids[None, :] % nfft).astype(jnp.float32) * angle_step
    alternate = (1 - 2 * (sample_ids % 2)).astype(jnp.float32)
    sine_part = jnp.where(bin_ids[None, :] == 0, alternate[:, None], -jnp.sin(phase))
    forward_table = jnp.concatenate([jnp.cos(phase), sine_part], axis=1)
    lag_ids = jnp.arange(lags, dtype=jnp.int32) - half_lags
    lag_phase = (bin_ids[:, None] * lag_ids[None, :] % nfft).astype(jnp.float32) * angle_step
    weights = jnp.where(bin_ids == 0, 1.0, 2.0).astype(jnp.float32)[:, None]
    scale_factor = 1.0 / (nfft * math.sqrt(samples))
    sign_row = (1 - 2 * (lag_ids % 2)).astype(jnp.float32)[None, :]
    cos_rows = weights * jnp.cos(lag_phase) * scale_factor
    sin_ahead = jnp.where(bin_ids[:, None] == 0, sign_row, -2.0 * jnp.sin(lag_phase)) * scale_factor
    sin_behind = jnp.where(bin_ids[:, None] == 0, sign_row, 2.0 * jnp.sin(lag_phase)) * scale_factor
    inverse_table = jnp.concatenate([cos_rows, sin_ahead], axis=0)
    reverse_table = jnp.concatenate([cos_rows, sin_behind], axis=0)
    return (forward_table, inverse_table, reverse_table)


def cross_spectrum(first, second):
    half_bins = first.shape[-1] // 2
    first_re = first[..., :half_bins]
    first_im = first[..., half_bins:]
    second_re = second[..., :half_bins]
    second_im = second[..., half_bins:]
    beyond_zero = (jnp.arange(half_bins) > 0).astype(first.dtype)
    real_part = first_re * second_re + beyond_zero * first_im * second_im
    imag_part = (
        beyond_zero * (first_re * second_im - first_im * second_re)
        + (1 - beyond_zero) * first_im * second_im
    )
    return jnp.concatenate([real_part, imag_part], axis=-1)


def local(traces, pair_first, pair_second, pair_valid):
    events = traces.shape[2]
    channels = traces.shape[3]
    samples = traces.shape[4]
    slot_count = pair_first.shape[3]
    forward_table, inverse_table, reverse_table = make_tables(samples, NFFT, LAGS)
    level = lax.Precision.HIGH
    nearby = with_halo(traces, (("wide", 0), ("narrow", 1)), 1)
    leading = nearby.shape[:-1]
    signal = nearby.reshape(-1, samples).astype(jnp.float32)
    spectra = jnp.dot(signal, forward_table, precision=level).reshape(leading + (NFFT,))
    spectra = spectra.reshape(9 * events, channels, NFFT)
    own_spec = spectra[4 * events : 5 * events]
    direction = jnp.arange(9, dtype=jnp.int32)[:, None]
    event_ids = jnp.arange(events, dtype=jnp.int32)
    firsts = pair_first[0, 0]
    seconds = pair_second[0, 0]
    live_mask = pair_valid[0, 0].astype(jnp.float32)
    first_spec = jnp.take(own_spec, firsts.reshape(-1), axis=0)
    second_spec = jnp.take(spectra, (direction * events + seconds).reshape(-1), axis=0)
    products = cross_spectrum(first_spec, second_spec) * live_mask.reshape(-1, 1, 1)
    pick_first = (firsts.reshape(-1)[None, :] == event_ids[:, None]).astype(jnp.float32)
    ahead_sum = jnp.dot(
        pick_first, products.reshape(9 * slot_count, channels * NFFT), precision=level
    )
    pick_second = (seconds[:, None, :] == event_ids[None, :, None]).astype(jnp.float32)
    behind = jnp.einsum(
        "deb,dbf->def",
        pick_second,
        products.reshape(9, slot_count, channels * NFFT),
        precision=level,
    )
    echoes = jnp.dot(behind.reshape(-1, NFFT), reverse_table, precision=level).reshape(
        3, 3, events, channels, LAGS
    )
    from_left = passed_along(echoes[:, 2], "narrow", 1)
    from_right = passed_along(echoes[:, 0], "narrow", -1)
    column = echoes[:, 1] + from_left + from_right
    from_above = passed_along(column[2], "wide", 1)
    from_below = passed_along(column[0], "wide", -1)
    returned = column[1] + from_above + from_below
    result = (
        jnp.dot(ahead_sum.reshape(-1, NFFT), inverse_table, precision=level).reshape(
            events, channels, LAGS
        )
        + returned
    )
    return result[None, None]


def solution(mesh):
    in_specs = (
        P("wide", "narrow", None, None, None),
        P("wide", "narrow", None, None),
        P("wide", "narrow", None, None),
        P("wide", "narrow", None, None),
    )
    out_specs = P("wide", "narrow", None, None, None)
    return jax.shard_map(local, mesh=mesh, in_specs=in_specs, out_specs=out_specs, check_vma=False)
```

profile of v0, /device:TPU:1, one launch (start us, length us, event | category | flops | bytes accessed | tf_op | source)
XLA Modules:
  0.0 519.8 jit_solution(6292779504704754123)
XLA Ops:
  6.9 15.7 %collective-permute-done = bf16[1,1,64,24,512]{4,3,2,1,0:T(8,128)(2,1)S(1)} collective-permute-done((bf16[1,1,64,24,512]{4,3,2,1,0:T(8,128)(2,1)}, bf16[1,1,64,24,512]{4,3,2,1,0:T(8,128)(2,1)S(1)}, u32[]{:S(2)}, u32[]{:S(2)}) %collective-permute-start) | collective-permute-done | bytes 1572896 | tf_op jit(solution)/shard_map/ppermute | solution.py:20
  29.9 6.2 %collective-permute-start.2 = (bf16[3,1,64,24,512]{4,3,2,1,0:T(8,128)(2,1)}, bf16[3,1,64,24,512]{4,3,2,1,0:T(8,128)(2,1)}, u32[]{:S(2)}, u32[]{:S(2)}) collective-permute-start(bf16[3,1,64,24,512]{4,3,2,1,0:T(8,128)(2,1)} %constant_dynamic-update-slice_fusion), channel_id=1, source_target_pairs={{0,1},{1,2},{2,3},{4,5},{5,6},{6,7},{8,9},{9,10},{10,11},{12,13},{... | collective-permute-start | bytes 14155784 | tf_op jit(solution)/shard_map/ppermute | solution.py:20
  48.0 70.0 %collective-permute-done.3 = bf16[3,1,64,24,512]{4,3,2,1,0:T(8,128)(2,1)} collective-permute-done((bf16[3,1,64,24,512]{4,3,2,1,0:T(8,128)(2,1)}, bf16[3,1,64,24,512]{4,3,2,1,0:T(8,128)(2,1)}, u32[]{:S(2)}, u32[]{:S(2)}) %collective-permute-start.3) | collective-permute-done | bytes 4718624 | tf_op jit(solution)/shard_map/ppermute | solution.py:22
  119.7 6.6 %pad_maximum_fusion.1 = bf16[3,3,64,24,512]{4,3,2,1,0:T(8,128)(2,1)S(1)} fusion(bf16[3,1,64,24,512]{4,3,2,1,0:T(8,128)(2,1)} %collective-permute-done.3, bf16[3,1,64,24,512]{4,3,2,1,0:T(8,128)(2,1)} %constant_dynamic-update-slice_fusion, bf16[3,1,64,24,512]{4,3,2,1,0:T(8,128)(2,1)} %collective-permute-done.2), kind=kLoop, calls=%fused_computation.10 | loop fusion | flops 14155776 | bytes 28311552 | tf_op jit(solution)/shard_map/concatenate | solution.py:18
  126.4 26.8 %fusion.14 = f32[13824,640]{1,0:T(8,128)} fusion(bf16[13824,512]{1,0:T(8,128)(2,1)S(1)} %bitcast.66, f32[512,320]{1,0:T(8,128)S(1)} %negate_select_fusion, f32[512,320]{1,0:T(8,128)S(1)} %fusion.22), kind=kOutput, calls=%fused_computation.29 | convolution fusion | flops 27179417600 | bytes 50855936 | tf_op jit(solution)/shard_map/dot_general | solution.py:83
  157.4 15.4 %gather_fusion = f32[288,24,640]{2,1,0:T(8,128)} fusion(f32[64,24,640]{2,1,0:T(8,128)} %bitcast.62, s32[1024]{0:T(1024)S(1)} %get-tuple-element.15), kind=kCustom, calls=%fused_computation | custom fusion | bytes 35390592 | tf_op jit(solution)/shard_map/jit(_take)/gather | solution.py:91
  172.8 12.1 %broadcast_select_fusion.1 = f32[288,24,640]{2,1,0:T(8,128)} fusion(f32[288,24,640]{2,1,0:T(8,128)} %gather_fusion, pred[288]{0:T(512)(128)(4,1)S(1)} %compare_and_fusion.1), kind=kLoop, calls=%fused_computation.16 | loop fusion | flops 4423680 | bytes 35389728 | tf_op jit(solution)/shard_map/jit(_take)/select_n | solution.py:91
  185.0 20.9 %gather_fusion.1 = f32[288,24,640]{2,1,0:T(8,128)} fusion(f32[576,24,640]{2,1,0:T(8,128)} %bitcast.63, s32[1024]{0:T(1024)S(1)} %get-tuple-element.14), kind=kCustom, calls=%fused_computation.1 | custom fusion | bytes 35390592 | tf_op jit(solution)/shard_map/jit(_take)/gather | solution.py:92
  205.9 12.2 %broadcast_select_fusion = f32[288,24,640]{2,1,0:T(8,128)} fusion(f32[288,24,640]{2,1,0:T(8,128)} %gather_fusion.1, pred[288]{0:T(512)(128)(4,1)S(1)} %compare_and_fusion), kind=kLoop, calls=%fused_computation.15 | loop fusion | flops 4423680 | bytes 35389728 | tf_op jit(solution)/shard_map/jit(_take)/select_n | solution.py:92
  218.1 19.6 %multiply_add_fusion.1 = (f32[288,24,320]{2,1,0:T(8,128)S(1)}, f32[288,24,320]{2,1,0:T(8,128)}) fusion(f32[288,24,640]{2,1,0:T(8,128)} %broadcast_select_fusion, f32[288,24,640]{2,1,0:T(8,128)} %broadcast_select_fusion.1, f32[320]{0:T(512)S(1)} %fusion.47, f32[320]{0:T(512)S(1)} %broadcast_subtract_fusion), kind=kLoop, calls=%fused_computation.12 | loop fusion | flops 24330240 | bytes 53086720 | tf_op jit(solution)/shard_map/add | solution.py:65
  237.7 11.4 %pad_maximum_fusion = f32[288,24,640]{2,1,0:T(8,128)} fusion(f32[288,24,320]{2,1,0:T(8,128)} %get-tuple-element.6, f32[288,24,320]{2,1,0:T(8,128)S(1)} %get-tuple-element.5), kind=kLoop, calls=%fused_computation.7 | loop fusion | flops 4423680 | bytes 35389440 | tf_op jit(solution)/shard_map/concatenate | solution.py:70
  249.2 16.7 %concatenate.28 = f32[9,32,15360]{2,1,0:T(8,128)} reshape(f32[288,24,640]{2,1,0:T(8,128)} %pad_maximum_fusion) | data formatting | bytes 35389440 | tf_op jit(solution)/shard_map/concatenate | solution.py:70
  265.9 19.8 %fusion.5 = f32[9,64,15360]{2,1,0:T(8,128)} fusion(f32[9,32,15360]{2,1,0:T(8,128)} %concatenate.28, f32[9,32]{1,0:T(8,128)S(1)} %bitcast.68, s32[9,32]{1,0:T(8,128)S(1)} %bitcast.67), kind=kOutput, calls=%fused_computation.8 | convolution fusion | flops 1703135232 | bytes 53086464 | tf_op jit(solution)/shard_map/deb,dbf->def/dot_general | solution.py:99
  285.6 31.8 %copy.19 = f32[72,8,24,640]{3,2,1,0:T(8,128)} copy(f32[72,8,24,640]{3,1,2,0:T(8,128)} %bitcast.59) | data formatting | bytes 70778880
  317.4 24.3 %fusion = f32[3,3,64,24,256]{4,3,2,0,1:T(8,128)} fusion(f32[3,3,64,24,640]{4,3,2,1,0:T(8,128)} %bitcast.61, f32[320,256]{1,0:T(8,128)S(1)} %get-tuple-element.13, f32[320,256]{1,0:T(8,128)S(1)} %get-tuple-element.12), kind=kOutput, calls=%fused_computation.2 | convolution fusion | flops 13589708800 | bytes 50200576 | tf_op jit(solution)/shard_map/dot_general | solution.py:105
  341.7 8.5 %slice_bitcast_fusion.1 = (f32[3,64,24,256]{3,2,1,0:T(8,128)}, f32[3,64,24,256]{3,2,1,0:T(8,128)}) fusion(f32[3,3,64,24,256]{4,3,2,0,1:T(8,128)} %fusion), kind=kLoop, calls=%fused_computation.18 | loop fusion | bytes 18874368 | tf_op jit(solution)/shard_map/squeeze | solution.py:108
  350.2 6.4 %collective-permute-start.4 = (f32[3,64,24,256]{3,2,1,0:T(8,128)}, f32[3,64,24,256]{3,2,1,0:T(8,128)}, u32[]{:S(2)}, u32[]{:S(2)}) collective-permute-start(f32[3,64,24,256]{3,2,1,0:T(8,128)} %get-tuple-element.7), channel_id=1, source_target_pairs={{0,1},{1,2},{2,3},{4,5},{5,6},{6,7},{8,9},{9,10},{10,11},{12,13},{... | collective-permute-start | bytes 14155784 | tf_op jit(solution)/shard_map/ppermute | solution.py:32
  358.0 9.8 %copy.18 = f32[36,8,24,640]{3,1,2,0:T(8,128)S(1)} copy(f32[36,8,24,640]{3,2,1,0:T(8,128)} %bitcast.60) | data formatting | bytes 35389440
  367.8 73.5 %collective-permute-done.4 = f32[3,64,24,256]{3,2,1,0:T(8,128)} collective-permute-done((f32[3,64,24,256]{3,2,1,0:T(8,128)}, f32[3,64,24,256]{3,2,1,0:T(8,128)}, u32[]{:S(2)}, u32[]{:S(2)}) %collective-permute-start.4) | collective-permute-done | bytes 4718624 | tf_op jit(solution)/shard_map/ppermute | solution.py:32
  441.2 6.3 %collective-permute-done.5 = f32[3,64,24,256]{3,2,1,0:T(8,128)} collective-permute-done((f32[3,64,24,256]{3,2,1,0:T(8,128)}, f32[3,64,24,256]{3,2,1,0:T(8,128)}, u32[]{:S(2)}, u32[]{:S(2)}) %collective-permute-start.5) | collective-permute-done | bytes 4718624 | tf_op jit(solution)/shard_map/ppermute | solution.py:32
  447.5 8.2 %fusion.9 = f32[3,64,24,256]{3,2,1,0:T(8,128)} fusion(f32[3,64,24,256]{3,2,1,0:T(8,128)} %collective-permute-done.5, f32[3,64,24,256]{3,2,1,0:T(8,128)} %collective-permute-done.4, f32[3,3,64,24,256]{4,3,2,0,1:T(8,128)} %fusion), kind=kLoop, calls=%fused_computation.21 | loop fusion | flops 2359296 | bytes 18874368 | tf_op jit(solution)/shard_map/add | solution.py:110
  459.6 33.3 %collective-permute-start.6 = (f32[64,24,256]{2,1,0:T(8,128)}, f32[64,24,256]{2,1,0:T(8,128)}, u32[]{:S(2)}, u32[]{:S(2)}) collective-permute-start(f32[64,24,256]{2,1,0:T(8,128)} %get-tuple-element.9), channel_id=1, source_target_pairs={{0,4},{4,8},{8,12},{12,16},{16,20},{20,24},{24,28},{28,32},{32,36}... | collective-permute-start | bytes 4718600 | tf_op jit(solution)/shard_map/ppermute | solution.py:32
  494.8 6.7 %broadcast_multiply_fusion = f32[288,15360]{1,0:T(8,128)} fusion(f32[288,15360]{1,0:T(8,128)S(1)} %bitcast.64, f32[288]{0:T(512)S(1)} %convert_element_type.65), kind=kLoop, calls=%fused_computation.14 | loop fusion | flops 4423680 | bytes 35390592 | tf_op jit(solution)/shard_map/mul | solution.py:93
  501.6 8.5 %fusion.2 = f32[64,24,640]{2,0,1:T(8,128)S(1)} fusion(f32[36,24,8,640]{3,2,1,0:T(8,128)} %bitcast.65, s32[288]{0:T(512)S(1)} %copy-done.2), kind=kOutput, calls=%fused_computation.4 | convolution fusion | flops 1698711552 | bytes 21628032 | tf_op jit(solution)/shard_map/dot_general | solution.py:95
  (53 shorter events, 48.6 us)
Async XLA Ops:
  0.0 22.6 %collective-permute-start = (bf16[1,1,64,24,512]{4,3,2,1,0:T(8,128)(2,1)}, bf16[1,1,64,24,512]{4,3,2,1,0:T(8,128)(2,1)S(1)}, u32[]{:S(2)}, u32[]{:S(2)}) collective-permute-start(bf16[1,1,64,24,512]{4,3,2,1,0:T(8,128)(2,1)} %param.4), channel_id=1, source_target_pairs={{0,4},{4,8},{8,12},{12,16},{16,20},{20,24},{24,28},{28,32},{32,36}... | collective-permute-start | bytes 4718600 | tf_op jit(solution)/shard_map/ppermute | solution.py:20
  4.9 22.3 %collective-permute-start.1 = (bf16[1,1,64,24,512]{4,3,2,1,0:T(8,128)(2,1)}, bf16[1,1,64,24,512]{4,3,2,1,0:T(8,128)(2,1)S(1)}, u32[]{:S(2)}, u32[]{:S(2)}) collective-permute-start(bf16[1,1,64,24,512]{4,3,2,1,0:T(8,128)(2,1)} %param.4), channel_id=1, source_target_pairs={{4,0},{8,4},{12,8},{16,12},{20,16},{24,20},{28,24},{32,28},{36,32}... | collective-permute-start | bytes 4718600 | tf_op jit(solution)/shard_map/ppermute | solution.py:22
  28.6 89.4 %collective-permute-start.3 = (bf16[3,1,64,24,512]{4,3,2,1,0:T(8,128)(2,1)}, bf16[3,1,64,24,512]{4,3,2,1,0:T(8,128)(2,1)}, u32[]{:S(2)}, u32[]{:S(2)}) collective-permute-start(bf16[3,1,64,24,512]{4,3,2,1,0:T(8,128)(2,1)} %constant_dynamic-update-slice_fusion), channel_id=1, source_target_pairs={{1,0},{2,1},{3,2},{5,4},{6,5},{7,6},{9,8},{10,9},{11,10},{13,12},{... | collective-permute-start | bytes 14155784 | tf_op jit(solution)/shard_map/ppermute | solution.py:22
  29.9 89.8 %collective-permute-start.2 = (bf16[3,1,64,24,512]{4,3,2,1,0:T(8,128)(2,1)}, bf16[3,1,64,24,512]{4,3,2,1,0:T(8,128)(2,1)}, u32[]{:S(2)}, u32[]{:S(2)}) collective-permute-start(bf16[3,1,64,24,512]{4,3,2,1,0:T(8,128)(2,1)} %constant_dynamic-update-slice_fusion), channel_id=1, source_target_pairs={{0,1},{1,2},{2,3},{4,5},{5,6},{6,7},{8,9},{9,10},{10,11},{12,13},{... | collective-permute-start | bytes 14155784 | tf_op jit(solution)/shard_map/ppermute | solution.py:20
  37.1 8.4 %copy-start.1 = (s32[288]{0:T(512)}, s32[288]{0:T(512)S(1)}, u32[]{:S(2)}) copy-start(s32[288]{0:T(512)S(1)} %eq.68) | copy-start | bytes 3460
  341.7 16.1 %copy-start.3 = (s32[1,1,9,32]{3,1,2,0:T(1,128)S(1)}, s32[1,1,9,32]{3,1,2,0:T(1,128)}, u32[]{:S(2)}) copy-start(s32[1,1,9,32]{3,1,2,0:T(1,128)} %param.7) | copy-start | bytes 3460
  350.2 91.0 %collective-permute-start.4 = (f32[3,64,24,256]{3,2,1,0:T(8,128)}, f32[3,64,24,256]{3,2,1,0:T(8,128)}, u32[]{:S(2)}, u32[]{:S(2)}) collective-permute-start(f32[3,64,24,256]{3,2,1,0:T(8,128)} %get-tuple-element.7), channel_id=1, source_target_pairs={{0,1},{1,2},{2,3},{4,5},{5,6},{6,7},{8,9},{9,10},{10,11},{12,13},{... | collective-permute-start | bytes 14155784 | tf_op jit(solution)/shard_map/ppermute | solution.py:32
  356.6 91.0 %collective-permute-start.5 = (f32[3,64,24,256]{3,2,1,0:T(8,128)}, f32[3,64,24,256]{3,2,1,0:T(8,128)}, u32[]{:S(2)}, u32[]{:S(2)}) collective-permute-start(f32[3,64,24,256]{3,2,1,0:T(8,128)} %get-tuple-element.8), channel_id=1, source_target_pairs={{1,0},{2,1},{3,2},{5,4},{6,5},{7,6},{9,8},{10,9},{11,10},{13,12},{... | collective-permute-start | bytes 14155784 | tf_op jit(solution)/shard_map/ppermute | solution.py:32
  459.6 52.6 %collective-permute-start.6 = (f32[64,24,256]{2,1,0:T(8,128)}, f32[64,24,256]{2,1,0:T(8,128)}, u32[]{:S(2)}, u32[]{:S(2)}) collective-permute-start(f32[64,24,256]{2,1,0:T(8,128)} %get-tuple-element.9), channel_id=1, source_target_pairs={{0,4},{4,8},{8,12},{12,16},{16,20},{20,24},{24,28},{28,32},{32,36}... | collective-permute-start | bytes 4718600 | tf_op jit(solution)/shard_map/ppermute | solution.py:32
  492.9 22.1 %collective-permute-start.7 = (f32[64,24,256]{2,1,0:T(8,128)}, f32[64,24,256]{2,1,0:T(8,128)}, u32[]{:S(2)}, u32[]{:S(2)}) collective-permute-start(f32[64,24,256]{2,1,0:T(8,128)} %get-tuple-element.10), channel_id=1, source_target_pairs={{4,0},{8,4},{12,8},{16,12},{20,16},{24,20},{28,24},{32,28},{36,32}... | collective-permute-start | bytes 4718600 | tf_op jit(solution)/shard_map/ppermute | solution.py:32
  494.8 6.7 %copy-start.2 = (s32[288]{0:T(512)S(1)}, s32[288]{0:T(512)}, u32[]{:S(2)}) copy-start(s32[288]{0:T(512)} %copy-done.1) | copy-start | bytes 3460
  501.6 8.5 %copy-start = (f32[320,256]{1,0:T(8,128)S(1)}, f32[320,256]{1,0:T(8,128)}, u32[]{:S(2)}) copy-start(f32[320,256]{1,0:T(8,128)} %get-tuple-element.11) | copy-start | bytes 983044
where the time goes:
time: 527 us; the launch traced here: 520 us
  waiting for transfers between devices  171 us (32%)
  local copies, waits for them, and re-layouts  118 us (22%)
  other arithmetic  92.2 us (17%)
  matrix products  81.4 us (15%)
  starting transfers between devices  57.2 us (11%)
    ppermute x4, waiting for transfers between devices, passed_along(): return lax.ppermute(x, axis, pairs)  82.5 us
    ppermute x2, waiting for transfers between devices, with_halo(): lax.ppermute(head, axis, [((i + 1) % count, i) for i in range(ends)])  70.7 us
    unnamed x14, local copies, waits for them, and re-layouts  46.2 us
    ppermute x4, starting transfers between devices, passed_along(): return lax.ppermute(x, axis, pairs)  42.9 us
    dot_general x1, matrix products, local(): jnp.dot(signal, forward_table, precision=level).reshape(leading + (NFFT,))  26.8 us
    dot_general x1, matrix products, local(): jnp.dot(behind.reshape(-1, NFFT), reverse_table, precision=level)  24.3 us
    gather x1, local copies, waits for them, and re-layouts, local(): jnp.take(spectra, (direction * events + seconds).reshape(-1), axis=0)  20.9 us
    dot_general x1, matrix products, local(): jnp.einsum('deb,dbf->def', pick_second, products.reshape(9, slot_count, c...  19.8 us
  transfers between devices with their start and end apart: 8, of which 7 were waited for; matrix products, arithmetic and copies ran while one was open for 8% of the time, Pallas kernels for 0%

commit v1 on v0

v1 whole, which is shorter than its diff:
```python
import functools
import math

import jax
import jax.numpy as jnp
import ml_dtypes
import numpy as np
from jax import lax
from jax.experimental import pallas as pl
from jax.experimental.pallas import tpu as pltpu
from jax.sharding import PartitionSpec as P

LAGS = 256
NFFT = 768
BLOCKS = 3
BINS = 128
CHUNK = 2
LAG = 2
WINDOW = 3
MESH = pl.DeviceIdType.MESH
F32 = jnp.float32
BF16 = jnp.bfloat16


def split_np(table):
    high = table.astype(ml_dtypes.bfloat16)
    low = (table - high.astype(np.float64)).astype(ml_dtypes.bfloat16)
    return np.stack([high, low])


def make_tables(samples):
    freq = np.arange(NFFT // 2, dtype=np.float64) + 0.5
    step = 2.0 * math.pi / NFFT
    phase = np.arange(samples, dtype=np.float64)[:, None] * freq[None, :] * step
    parts = []
    for b in range(BLOCKS):
        cols = slice(b * BINS, (b + 1) * BINS)
        parts += [np.cos(phase[:, cols]), -np.sin(phase[:, cols])]
    forward = np.concatenate(parts, axis=1)
    lag = np.arange(LAGS, dtype=np.float64) - LAGS // 2
    phase = freq[:, None] * lag[None, :] * step
    scale = 2.0 / (NFFT * math.sqrt(samples))
    parts = []
    for b in range(BLOCKS):
        rows = slice(b * BINS, (b + 1) * BINS)
        parts += [np.cos(phase[rows]) * scale, -np.sin(phase[rows]) * scale]
    return split_np(forward), split_np(np.concatenate(parts, axis=0))


def split(v):
    high = v.astype(BF16)
    return high, (v - high.astype(F32)).astype(BF16)


def dot(a, b):
    return jnp.dot(a, b, preferred_element_type=F32)


def kernel(
    traces, first, second, valid, fwd_hbm, inv_hbm, out,
    raw, wide32, cells, part_up, part_own, part_down, got_up, got_down,
    weights, codes, fwd, inv, held,
    load_sem, table_sem, code_send, code_recv,
    x_send_left, x_send_right, x_from_left, x_from_right,
    y_send_up, y_send_down, y_from_up, y_from_down, out_sem,
):
    events, channels, samples = traces.shape
    lanes = samples // 128
    chunks = channels // CHUNK
    rows, cols = lax.axis_size("wide"), lax.axis_size("narrow")
    row, col = lax.axis_index("wide"), lax.axis_index("narrow")
    left = {"narrow": lax.rem(col + cols - 1, cols)}
    right = {"narrow": lax.rem(col + 1, cols)}
    up = {"wide": lax.rem(row + rows - 1, rows)}
    down = {"wide": lax.rem(row + 1, rows)}

    load = pltpu.make_async_copy(traces, raw, load_sem)
    load.start()
    load_fwd = pltpu.make_async_copy(fwd_hbm, fwd, table_sem.at[0])
    load_inv = pltpu.make_async_copy(inv_hbm, inv, table_sem.at[1])
    load_fwd.start()
    load_inv.start()

    barrier = pltpu.get_barrier_semaphore()
    for peer in (left, right, up, down):
        pl.semaphore_signal(barrier, inc=1, device_id=peer, device_id_type=MESH)

    slots = first.shape[1]
    codes[0, 0:9, 0:slots] = jnp.where(
        valid[...] == 1, first[...] * events + second[...], -1
    )
    pl.semaphore_wait(barrier, 4)

    def remote(src, dst, send, recv, peer):
        return pltpu.make_async_remote_copy(
            src_ref=src, dst_ref=dst, send_sem=send, recv_sem=recv,
            device_id=peer, device_id_type=MESH,
        )

    code_copies = [
        remote(codes.at[0], codes.at[slot], code_send.at[slot - 1], code_recv.at[slot - 1], peer)
        for slot, peer in ((1, right), (2, left), (3, down), (4, up))
    ]
    for copy in code_copies:
        copy.start()

    def x_left(k):
        block = pl.ds(k * CHUNK, CHUNK)
        return remote(
            cells.at[block, events : 2 * events, :], cells.at[block, 2 * events : 3 * events, :],
            x_send_left.at[k], x_from_right.at[k], left,
        )

    def x_right(k):
        block = pl.ds(k * CHUNK, CHUNK)
        return remote(
            cells.at[block, events : 2 * events, :], cells.at[block, 0:events, :],
            x_send_right.at[k], x_from_left.at[k], right,
        )

    def y_up(k):
        block = pl.ds(k * CHUNK, CHUNK)
        return remote(
            part_up.at[block], got_down.at[block], y_send_up.at[k], y_from_down.at[k], up
        )

    def y_down(k):
        block = pl.ds(k * CHUNK, CHUNK)
        return remote(
            part_down.at[block], got_up.at[block], y_send_down.at[k], y_from_up.at[k], down
        )

    load.wait()
    for i in range(lanes):
        spread = raw[:, :, i * 128 : (i + 1) * 128].astype(F32)
        wide32[i] = spread.reshape(events * channels, 128)

    def turn(k, _):
        for n in range(CHUNK):
            c = k * CHUNK + n
            for i in range(lanes):
                lane_block = wide32[i, pl.ds(c, events, stride=channels), :]
                cells[c, events : 2 * events, i * 128 : (i + 1) * 128] = lane_block.astype(BF16)

        @pl.when(k < WINDOW)
        def _():
            x_left(k).start()
            x_right(k).start()

        return 0

    lax.fori_loop(0, chunks, turn, 0)

    for copy in code_copies:
        copy.wait()

    ids = lax.broadcasted_iota(jnp.int32, (events, slots), 0)

    def ends(slot, heading):
        code = codes[slot, heading : heading + 1, 0:slots]
        live = code >= 0
        head = jnp.where(live, code // events, -1)
        tail = jnp.where(live, code % events, -1)
        return (
            jnp.where(ids == head, 1.0, 0.0).astype(BF16),
            jnp.where(ids == tail, 1.0, 0.0).astype(BF16),
        )

    def outer(a, b):
        return lax.dot_general(
            a, b, (((1,), (1,)), ((), ())), preferred_element_type=F32
        )

    for i in (-1, 0, 1):
        target = {-1: 3, 0: 0, 1: 4}[i]
        for j in (-1, 0, 1):
            source = {-1: 1, 0: 0, 1: 2}[j]
            head, tail = ends(target, (1 - i) * 3 + (j + 1))
            count = outer(head, tail)
            head, tail = ends(source, (i + 1) * 3 + (1 - j))
            count = count + outer(tail, head)
            weights[
                (i + 1) * events : (i + 2) * events, (j + 1) * events : (j + 2) * events
            ] = count.astype(BF16)

    load_fwd.wait()
    load_inv.wait()

    def gather(k):
        x_left(k).wait()
        x_right(k).wait()

        @pl.when(k + WINDOW < chunks)
        def _():
            x_left(k + WINDOW).start()
            x_right(k + WINDOW).start()

        for n in range(CHUNK):
            c = k * CHUNK + n
            part = dot(weights[...], cells[c])
            part_up[c] = part[0:events]
            part_own[c] = part[events : 2 * events]
            part_down[c] = part[2 * events : 3 * events]
        y_up(k).start()
        y_down(k).start()

    def correlate(k):
        y_up(k).wait()
        y_down(k).wait()
        size = CHUNK * events
        block = pl.ds(k * CHUNK, CHUNK)
        x = cells[block, events : 2 * events, :].reshape(size, samples)
        y = (part_own[block] + got_up[block] + got_down[block]).reshape(size, samples)
        y_high, y_low = split(y)
        stack3 = jnp.concatenate([x, y_high, y_low], axis=0)
        stack2 = jnp.concatenate([x, y_high], axis=0)
        total = jnp.zeros((size, LAGS), F32)
        for b in range(BLOCKS):
            span = slice(b * 2 * BINS, (b + 1) * 2 * BINS)
            coarse = dot(stack3, fwd[0, :, span])
            fine = dot(stack2, fwd[1, :, span])
            xs = coarse[0:size] + fine[0:size]
            ys = coarse[size : 2 * size] + coarse[2 * size :] + fine[size:]
            xr, xi = xs[:, :BINS], xs[:, BINS:]
            yr, yi = ys[:, :BINS], ys[:, BINS:]
            s = jnp.concatenate([xr * yr + xi * yi, xr * yi - xi * yr], axis=1)
            s_high, s_low = split(s)
            both = dot(jnp.concatenate([s_high, s_low], axis=0), inv[0, span, :])
            total = total + (both[:size] + both[size:] + dot(s_high, inv[1, span, :]))
        for n in range(CHUNK):
            for i in range(LAGS // 128):
                held[i, pl.ds(k * CHUNK + n, events, stride=channels), :] = total[
                    n * events : (n + 1) * events, i * 128 : (i + 1) * 128
                ]

    def step(k, _):
        @pl.when(k < chunks)
        def _():
            gather(k)

        @pl.when(k >= LAG)
        def _():
            correlate(k - LAG)

        return 0

    lax.fori_loop(0, chunks + LAG, step, 0)
    stores = [
        pltpu.make_async_copy(held.at[i], out.at[:, i * 128 : (i + 1) * 128], out_sem.at[i])
        for i in range(LAGS // 128)
    ]
    for store in stores:
        store.start()
    for store in stores:
        store.wait()


def local(forward, inverse, traces, pair_first, pair_second, pair_valid):
    _, _, events, channels, samples = traces.shape
    chunks = channels // CHUNK
    part = pltpu.VMEM((channels, events, samples), F32)
    any_space = pl.BlockSpec(memory_space=pl.ANY)
    in_vmem = pl.BlockSpec(memory_space=pltpu.VMEM)
    dma = pltpu.SemaphoreType.DMA
    out = pl.pallas_call(
        kernel,
        out_shape=jax.ShapeDtypeStruct((events * channels, LAGS), F32),
        in_specs=[any_space, in_vmem, in_vmem, in_vmem, any_space, any_space],
        out_specs=any_space,
        scratch_shapes=[
            pltpu.VMEM((events, channels, samples), BF16),
            pltpu.VMEM((samples // 128, events * channels, 128), F32),
            pltpu.VMEM((channels, 3 * events, samples), BF16),
            part, part, part, part, part,
            pltpu.VMEM((3 * events, 3 * events), BF16),
            pltpu.VMEM((5, 16, 128), jnp.int32),
            pltpu.VMEM(forward.shape, BF16),
            pltpu.VMEM(inverse.shape, BF16),
            pltpu.VMEM((LAGS // 128, events * channels, 128), F32),
            dma, dma((2,)), dma((4,)), dma((4,)),
        ] + [dma((chunks,))] * 8 + [dma((LAGS // 128,))],
        compiler_params=pltpu.CompilerParams(
            collective_id=0, has_side_effects=True, vmem_limit_bytes=56 * 1024 * 1024
        ),
        cost_estimate=pl.CostEstimate(
            flops=8 * 10**9, bytes_accessed=6 * 10**6, transcendentals=0
        ),
        name="event_correlation",
    )(traces[0, 0], pair_first[0, 0], pair_second[0, 0], pair_valid[0, 0], forward, inverse)
    return out.reshape(1, 1, events, channels, LAGS)


def solution(mesh):
    forward, inverse = make_tables(512)
    spec4 = P("wide", "narrow", None, None)
    spec5 = P("wide", "narrow", None, None, None)

    def run(traces, pair_first, pair_second, pair_valid):
        return local(
            jnp.asarray(forward), jnp.asarray(inverse), traces, pair_first, pair_second, pair_valid
        )

    return jax.shard_map(
        run, mesh=mesh, in_specs=(spec5, spec4, spec4, spec4), out_specs=spec5, check_vma=False
    )
```

time: 527 us -> 60 us (0.11)
  the two profiles are of different devices: /device:TPU:1 before, /device:TPU:0 now
where the time goes in v1:
time: 60 us; the launch traced here: 59.8 us
  Pallas kernels  54.5 us (91%)
  local copies, waits for them, and re-layouts  5.25 us (9%)
    pallas_call x1, Pallas kernels, local(): pl.pallas_call(kernel, out_shape=jax.ShapeDtypeStruct((events * channels,...  54.5 us
    unnamed x3, local copies, waits for them, and re-layouts  5.25 us

profile of v1, /device:TPU:0, one launch (start us, length us, event | category | flops | bytes accessed | tf_op | source)
XLA Modules:
  0.0 59.8 jit_solution(4185532059754284703)
XLA Ops:
  0.0 1.3 %copy.13 = s32[1,1,9,32]{3,2,1,0:T(8,128)} copy(s32[1,1,9,32]{3,1,2,0:T(1,128)} %param.7) | data formatting | bytes 2304
  1.3 1.3 %copy_bitcast_fusion = (s32[9,32]{1,0:T(8,128)}, s32[9,32]{1,0:T(8,128)}) fusion(s32[1,1,9,32]{3,1,2,0:T(1,128)} %param.9, s32[1,1,9,32]{3,1,2,0:T(1,128)} %param.8), kind=kLoop, calls=%fused_computation | loop fusion | bytes 4608
  2.6 54.5 %event_correlation.1 = f32[1536,256]{1,0:T(8,128)} custom-call(bf16[64,24,512]{2,1,0:T(8,128)(2,1)} %bitcast.11, s32[9,32]{1,0:T(8,128)} %bitcast.10, s32[9,32]{1,0:T(8,128)} %get-tuple-element.6.second, s32[9,32]{1,0:T(8,128)} %get-tuple-element.5.valid, bf16[2,512,768]{2,1,0:T(8,128)(2,1)} %constant.4.clone.fwd_hbm, bf16[2,768,256]{2,1,0:T(8,128)(2,1)} %constant.5.clone.inv_hbm), custom_call_target="tpu_custom_call" | custom-call | flops 8000000000 | bytes 6000000 | tf_op jit(solution)/shard_map/event_correlation/pallas_call | solution.py:265
  57.1 2.7 %copy.15 = f32[1,1,64,24,256]{4,3,2,1,0:T(8,128)} copy(f32[1,1,64,24,256]{4,3,2,1,0:T(8,128)} %bitcast.9) | data formatting | bytes 3145728

commit v2 on v1

--- a/solution.py
+++ b/solution.py
@@ -16,7 +16,6 @@
 BINS = 128
 CHUNK = 2
 LAG = 2
-WINDOW = 3
 MESH = pl.DeviceIdType.MESH
 F32 = jnp.float32
 BF16 = jnp.bfloat16
@@ -62,7 +61,7 @@
     weights, codes, fwd, inv, held,
     load_sem, table_sem, code_send, code_recv,
     x_send_left, x_send_right, x_from_left, x_from_right,
-    y_send_up, y_send_down, y_from_up, y_from_down, out_sem,
+    y_send_up, y_send_down, y_from_up, y_from_down,
 ):
     events, channels, samples = traces.shape
     lanes = samples // 128
@@ -73,23 +72,59 @@
     right = {"narrow": lax.rem(col + 1, cols)}
     up = {"wide": lax.rem(row + rows - 1, rows)}
     down = {"wide": lax.rem(row + 1, rows)}
+    has_left, has_right = col > 0, col < cols - 1
+    has_up, has_down = row > 0, row < rows - 1
+    sides = ((has_left, left), (has_right, right), (has_up, up), (has_down, down))
 
     load = pltpu.make_async_copy(traces, raw, load_sem)
     load.start()
+    barrier = pltpu.get_barrier_semaphore()
+    for has, peer in sides:
+        @pl.when(has)
+        def _():
+            pl.semaphore_signal(barrier, inc=1, device_id=peer, device_id_type=MESH)
+
     load_fwd = pltpu.make_async_copy(fwd_hbm, fwd, table_sem.at[0])
     load_inv = pltpu.make_async_copy(inv_hbm, inv, table_sem.at[1])
     load_fwd.start()
     load_inv.start()
 
-    barrier = pltpu.get_barrier_semaphore()
-    for peer in (left, right, up, down):
-        pl.semaphore_signal(barrier, inc=1, device_id=peer, device_id_type=MESH)
-
-    slots = first.shape[1]
+    slots = first.shape[2]
     codes[0, 0:9, 0:slots] = jnp.where(
-        valid[...] == 1, first[...] * events + second[...], -1
+        valid[:, 0, :] == 1, first[:, 0, :] * events + second[:, 0, :], -1
     )
-    pl.semaphore_wait(barrier, 4)
+
+    def blank(has, slot, block, rows_from):
+        @pl.when(jnp.logical_not(has))
+        def _():
+            codes[slot] = jnp.full(codes.shape[1:], -1, jnp.int32)
+
+            def clear(c, _):
+                if rows_from is None:
+                    block[c] = jnp.zeros(block.shape[1:], block.dtype)
+                else:
+                    block[c, rows_from : rows_from + events, :] = jnp.zeros(
+                        (events, samples), block.dtype
+                    )
+                return 0
+
+            lax.fori_loop(0, channels, clear, 0)
+
+    blank(has_left, 1, cells, 0)
+    blank(has_right, 2, cells, 2 * events)
+    blank(has_up, 3, got_up, None)
+    blank(has_down, 4, got_down, None)
+
+    def turn(group):
+        for i in range(lanes):
+            spread = raw[:, group * 8 : (group + 1) * 8, i * 128 : (i + 1) * 128].astype(F32)
+            wide32[group, i] = spread.reshape(events * 8, 128)
+        for n in range(8):
+            for i in range(lanes):
+                lane_block = wide32[group, i, pl.ds(n, events, stride=8), :]
+                cells[group * 8 + n, events : 2 * events, i * 128 : (i + 1) * 128] = (
+                    lane_block.astype(BF16)
+                )
 
     def remote(src, dst, send, recv, peer):
         return pltpu.make_async_remote_copy(
@@ -99,10 +134,9 @@
 
     code_copies = [
         remote(codes.at[0], codes.at[slot], code_send.at[slot - 1], code_recv.at[slot - 1], peer)
-        for slot, peer in ((1, right), (2, left), (3, down), (4, up))
+        for slot, peer in ((2, left), (1, right), (4, up), (3, down))
     ]
-    for copy in code_copies:
-        copy.start()
+    has_from = {1: has_left, 2: has_right, 3: has_up, 4: has_down}
 
     def x_left(k):
         block = pl.ds(k * CHUNK, CHUNK)
@@ -130,29 +164,39 @@
             part_down.at[block], got_up.at[block], y_send_down.at[k], y_from_up.at[k], down
         )
 
+    def start_if(has, make):
+        @pl.when(has)
+        def _():
+            make().start()
+
+    def wait_send_if(has, make):
+        @pl.when(has)
+        def _():
+            make().wait_send()
+
+    def wait_recv_if(has, make):
+        @pl.when(has)
+        def _():
+            make().wait_recv()
+
+    def send_x(k):
+        start_if(has_left, lambda: x_left(k))
+        start_if(has_right, lambda: x_right(k))
+
     load.wait()
-    for i in range(lanes):
-        spread = raw[:, :, i * 128 : (i + 1) * 128].astype(F32)
-        wide32[i] = spread.reshape(events * channels, 128)
-
-    def turn(k, _):
-        for n in range(CHUNK):
-            c = k * CHUNK + n
-            for i in range(lanes):
-                lane_block = wide32[i, pl.ds(c, events, stride=channels), :]
-                cells[c, events : 2 * events, i * 128 : (i + 1) * 128] = lane_block.astype(BF16)
-
-        @pl.when(k < WINDOW)
-        def _():
-            x_left(k).start()
-            x_right(k).start()
-
-        return 0
-
-    lax.fori_loop(0, chunks, turn, 0)
-
-    for copy in code_copies:
-        copy.wait()
+    turn(0)
+    peers = sum(has.astype(jnp.int32) for has, _ in sides)
+    pl.semaphore_wait(barrier, peers)
+    for copy, (has, _) in zip(code_copies, sides):
+        start_if(has, lambda: copy)
+    for k in range(8 // CHUNK):
+        send_x(k)
+    for group in range(1, channels // 8):
+        turn(group)
+
+    for copy, slot, (has, _) in zip(code_copies, (2, 1, 4, 3), sides):
+        wait_send_if(has, lambda: copy)
+        wait_recv_if(has_from[slot], lambda: copy)
 
     ids = lax.broadcasted_iota(jnp.int32, (events, slots), 0)
 
@@ -187,13 +231,12 @@
     load_inv.wait()
 
     def gather(k):
-        x_left(k).wait()
-        x_right(k).wait()
-
-        @pl.when(k + WINDOW < chunks)
-        def _():
-            x_left(k + WINDOW).start()
-            x_right(k + WINDOW).start()
+        @pl.when(k + 8 // CHUNK < chunks)
+        def _():
+            send_x(k + 8 // CHUNK)
+
+        wait_recv_if(has_left, lambda: x_right(k))
+        wait_recv_if(has_right, lambda: x_left(k))
 
         for n in range(CHUNK):
             c = k * CHUNK + n
@@ -201,12 +244,12 @@
             part_up[c] = part[0:events]
             part_own[c] = part[events : 2 * events]
             part_down[c] = part[2 * events : 3 * events]
-        y_up(k).start()
-        y_down(k).start()
+        start_if(has_up, lambda: y_up(k))
+        start_if(has_down, lambda: y_down(k))
 
     def correlate(k):
-        y_up(k).wait()
-        y_down(k).wait()
+        wait_recv_if(has_up, lambda: y_down(k))
+        wait_recv_if(has_down, lambda: y_up(k))
         size = CHUNK * events
         block = pl.ds(k * CHUNK, CHUNK)
         x = cells[block, events : 2 * events, :].reshape(size, samples)
@@ -227,12 +270,19 @@
             s_high, s_low = split(s)
             both = dot(jnp.concatenate([s_high, s_low], axis=0), inv[0, span, :])
             total = total + (both[:size] + both[size:] + dot(s_high, inv[1, span, :]))
+        per_group = 8 // CHUNK
         for n in range(CHUNK):
             for i in range(LAGS // 128):
-                held[i, pl.ds(k * CHUNK + n, events, stride=channels), :] = total[
+                held[i, pl.ds(k % per_group * CHUNK + n, events, stride=8), :] = total[
                     n * events : (n + 1) * events, i * 128 : (i + 1) * 128
                 ]
 
+        @pl.when(k % per_group == per_group - 1)
+        def _():
+            place = pl.ds(pl.multiple_of(k // per_group * 8, 8), 8)
+            for i in range(LAGS // 128):
+                out[:, place, i * 128 : (i + 1) * 128] = held[i].reshape(events, 8, 128)
+
     def step(k, _):
         @pl.when(k < chunks)
         def _():
@@ -245,49 +295,53 @@
         return 0
 
     lax.fori_loop(0, chunks + LAG, step, 0)
-    stores = [
-        pltpu.make_async_copy(held.at[i], out.at[:, i * 128 : (i + 1) * 128], out_sem.at[i])
-        for i in range(LAGS // 128)
-    ]
-    for store in stores:
-        store.start()
-    for store in stores:
-        store.wait()
+    def finish(k, _):
+        wait_send_if(has_left, lambda: x_left(k))
+        wait_send_if(has_right, lambda: x_right(k))
+        wait_send_if(has_up, lambda: y_up(k))
+        wait_send_if(has_down, lambda: y_down(k))
+        return 0
+
+    lax.fori_loop(0, chunks, finish, 0)
+
+
+def by_heading(pairs):
+    return pairs.transpose(0, 2, 1, 3)[0]
 
 
 def local(forward, inverse, traces, pair_first, pair_second, pair_valid):
     _, _, events, channels, samples = traces.shape
     chunks = channels // CHUNK
     part = pltpu.VMEM((channels, events, samples), F32)
-    any_space = pl.BlockSpec(memory_space=pl.ANY)
+    in_hbm = pl.BlockSpec(memory_space=pltpu.HBM)
     in_vmem = pl.BlockSpec(memory_space=pltpu.VMEM)
     dma = pltpu.SemaphoreType.DMA
     out = pl.pallas_call(
         kernel,
-        out_shape=jax.ShapeDtypeStruct((events * channels, LAGS), F32),
-        in_specs=[any_space, in_vmem, in_vmem, in_vmem, any_space, any_space],
-        out_specs=any_space,
+        out_shape=jax.ShapeDtypeStruct((events, channels, LAGS), F32),
+        in_specs=[in_hbm, in_vmem, in_vmem, in_vmem, in_hbm, in_hbm],
+        out_specs=in_vmem,
         scratch_shapes=[
             pltpu.VMEM((events, channels, samples), BF16),
-            pltpu.VMEM((samples // 128, events * channels, 128), F32),
+            pltpu.VMEM((channels // 8, samples // 128, events * 8, 128), F32),
             pltpu.VMEM((channels, 3 * events, samples), BF16),
             part, part, part, part, part,
             pltpu.VMEM((3 * events, 3 * events), BF16),
             pltpu.VMEM((5, 16, 128), jnp.int32),
             pltpu.VMEM(forward.shape, BF16),
             pltpu.VMEM(inverse.shape, BF16),
-            pltpu.VMEM((LAGS // 128, events * channels, 128), F32),
+            pltpu.VMEM((LAGS // 128, events * 8, 128), F32),
             dma, dma((2,)), dma((4,)), dma((4,)),
-        ] + [dma((chunks,))] * 8 + [dma((LAGS // 128,))],
+        ] + [dma((chunks,))] * 8,
         compiler_params=pltpu.CompilerParams(
-            collective_id=0, has_side_effects=True, vmem_limit_bytes=56 * 1024 * 1024
+            collective_id=0, has_side_effects=True, vmem_limit_bytes=40 * 1024 * 1024
         ),
         cost_estimate=pl.CostEstimate(
             flops=8 * 10**9, bytes_accessed=6 * 10**6, transcendentals=0
         ),
         name="event_correlation",
-    )(traces[0, 0], pair_first[0, 0], pair_second[0, 0], pair_valid[0, 0], forward, inverse)
-    return out.reshape(1, 1, events, channels, LAGS)
+    )(*[pltpu.with_memory_space_constraint(v, pltpu.HBM) for v in (traces[0, 0], by_heading(pair_first), by_heading(pair_second), by_heading(pair_valid), forward, inverse)])
+    return out[None, None]
 
 
 def solution(mesh):

time: 60 us -> 50.5 us (0.84)
  the two profiles are of different devices: /device:TPU:0 before, /device:TPU:1 now
where the time goes in v2:
time: 50.5 us; the launch traced here: 50.1 us
  Pallas kernels  49 us (97%)
  local copies, waits for them, and re-layouts  1.15 us (2%)
    pallas_call x1, Pallas kernels, local(): pl.pallas_call(kernel, out_shape=jax.ShapeDtypeStruct((events, channels,...  49 us
    unnamed x1, local copies, waits for them, and re-layouts  1.15 us

profile of v2, /device:TPU:1, one launch (start us, length us, event | category | flops | bytes accessed | tf_op | source)
XLA Modules:
  0.0 50.1 jit_solution(11115585913252910132)
XLA Ops:
  0.0 49.0 %event_correlation.1 = f32[64,24,256]{2,1,0:T(8,128)S(1)} custom-call(bf16[64,24,512]{2,1,0:T(8,128)(2,1)} %bitcast.6, s32[9,1,32]{2,1,0:T(1,128)} %bitcast.7, s32[9,1,32]{2,1,0:T(1,128)} %bitcast.8, s32[9,1,32]{2,1,0:T(1,128)} %bitcast.9, bf16[2,512,768]{2,1,0:T(8,128)(2,1)} %constant.4.clone.fwd_hbm, bf16[2,768,256]{2,1,0:T(8,128)(2,1)} %constant.5.clone.inv_hbm), custom_call_target="tpu_custom_call" | custom-call | flops 8000000000 | bytes 6000000 | tf_op jit(solution)/shard_map/event_correlation/pallas_call | solution.py:319
  49.0 1.1 %copy.8 = f32[1,1,64,24,256]{4,3,2,1,0:T(8,128)} copy(f32[1,1,64,24,256]{4,3,2,1,0:T(8,128)S(1)} %bitcast.5) | data formatting | bytes 3145728

commit v3 on v2

--- a/solution.py
+++ b/solution.py
@@ -16,6 +16,7 @@
 BINS = 128
 CHUNK = 2
 LAG = 2
+CODE_MAX = 32767.0
 MESH = pl.DeviceIdType.MESH
 F32 = jnp.float32
 BF16 = jnp.bfloat16
@@ -57,7 +58,7 @@
 
 def kernel(
     traces, first, second, valid, fwd_hbm, inv_hbm, out,
-    raw, wide32, cells, part_up, part_own, part_down, got_up, got_down,
+    raw, wide32, cells, part_own, sent_up, sent_down, got_up, got_down,
     weights, codes, fwd, inv, held,
     load_sem, table_sem, code_send, code_recv,
     x_send_left, x_send_right, x_from_left, x_from_right,
@@ -94,26 +95,23 @@
         valid[:, 0, :] == 1, first[:, 0, :] * events + second[:, 0, :], -1
     )
 
-    def blank(has, slot, block, rows_from):
+    def blank(has, slot, block, first_row, row_count):
         @pl.when(jnp.logical_not(has))
         def _():
             codes[slot] = jnp.full(codes.shape[1:], -1, jnp.int32)
 
-            def clear(c, _):
-                if rows_from is None:
-                    block[c] = jnp.zeros(block.shape[1:], block.dtype)
-                else:
-                    block[c, rows_from : rows_from + events, :] = jnp.zeros(
-                        (events, samples), block.dtype
-                    )
+            def clear(n, _):
+                block[n, first_row : first_row + row_count, :] = jnp.zeros(
+                    (row_count, samples), block.dtype
+                )
                 return 0
 
-            lax.fori_loop(0, channels, clear, 0)
-
-    blank(has_left, 1, cells, 0)
-    blank(has_right, 2, cells, 2 * events)
-    blank(has_up, 3, got_up, None)
-    blank(has_down, 4, got_down, None)
+            lax.fori_loop(0, block.shape[0], clear, 0)
+
+    blank(has_left, 1, cells, 0, events)
+    blank(has_right, 2, cells, 2 * events, events)
+    blank(has_up, 3, got_up, 0, got_up.shape[1])
+    blank(has_down, 4, got_down, 0, got_down.shape[1])
 
     def turn(group):
         for i in range(lanes):
@@ -153,16 +151,10 @@
         )
 
     def y_up(k):
-        block = pl.ds(k * CHUNK, CHUNK)
-        return remote(
-            part_up.at[block], got_down.at[block], y_send_up.at[k], y_from_down.at[k], up
-        )
+        return remote(sent_up.at[k], got_down.at[k], y_send_up.at[k], y_from_down.at[k], up)
 
     def y_down(k):
-        block = pl.ds(k * CHUNK, CHUNK)
-        return remote(
-            part_down.at[block], got_up.at[block], y_send_down.at[k], y_from_up.at[k], down
-        )
+        return remote(sent_down.at[k], got_up.at[k], y_send_down.at[k], y_from_up.at[k], down)
 
     def start_if(has, make):
         @pl.when(has)
@@ -230,6 +222,27 @@
     load_fwd.wait()
     load_inv.wait()
 
+    size = CHUNK * events
+    diagonal = lax.broadcasted_iota(jnp.int32, (size, size), 0) == lax.broadcasted_iota(
+        jnp.int32, (size, size), 1
+    )
+
+    def encode(ref, k, part):
+        peak = jnp.max(jnp.abs(part), axis=1, keepdims=True)
+        power = jnp.ceil(jnp.log2(jnp.maximum(peak, 1e-30)) + 1e-4)
+        code = jnp.round(part * (jnp.exp2(-power) * CODE_MAX))
+        ref[k, 0:size, :] = code.astype(jnp.int32).astype(jnp.int16)
+        band = jnp.sum(jnp.where(diagonal, power, 0.0), axis=0, keepdims=True)
+        ref[k, size : size + 16, 0:size] = (
+            jnp.broadcast_to(band, (16, size)).astype(jnp.int32).astype(jnp.int16)
+        )
+
+    def decode(ref, k):
+        band = ref[k, size : size + 16, 0:size].astype(jnp.int32).astype(F32)[0:1]
+        power = jnp.sum(jnp.where(diagonal, band, 0.0), axis=1, keepdims=True)
+        code = ref[k, 0:size, :].astype(jnp.int32).astype(F32)
+        return code * (jnp.exp2(power) * (1.0 / CODE_MAX))
+
     def gather(k):
         @pl.when(k + 8 // CHUNK < chunks)
         def _():
@@ -238,22 +251,20 @@
         wait_recv_if(has_left, lambda: x_right(k))
         wait_recv_if(has_right, lambda: x_left(k))
 
+        parts = [dot(weights[...], cells[k * CHUNK + n]) for n in range(CHUNK)]
         for n in range(CHUNK):
-            c = k * CHUNK + n
-            part = dot(weights[...], cells[c])
-            part_up[c] = part[0:events]
-            part_own[c] = part[events : 2 * events]
-            part_down[c] = part[2 * events : 3 * events]
+            part_own[k * CHUNK + n] = parts[n][events : 2 * events]
+        encode(sent_up, k, jnp.concatenate([p[0:events] for p in parts], axis=0))
+        encode(sent_down, k, jnp.concatenate([p[2 * events :] for p in parts], axis=0))
         start_if(has_up, lambda: y_up(k))
         start_if(has_down, lambda: y_down(k))
 
     def correlate(k):
         wait_recv_if(has_up, lambda: y_down(k))
         wait_recv_if(has_down, lambda: y_up(k))
-        size = CHUNK * events
         block = pl.ds(k * CHUNK, CHUNK)
         x = cells[block, events : 2 * events, :].reshape(size, samples)
-        y = (part_own[block] + got_up[block] + got_down[block]).reshape(size, samples)
+        y = part_own[block].reshape(size, samples) + decode(got_up, k) + decode(got_down, k)
         y_high, y_low = split(y)
         stack3 = jnp.concatenate([x, y_high, y_low], axis=0)
         stack2 = jnp.concatenate([x, y_high], axis=0)
@@ -313,6 +324,7 @@
     _, _, events, channels, samples = traces.shape
     chunks = channels // CHUNK
     part = pltpu.VMEM((channels, events, samples), F32)
+    code = pltpu.VMEM((chunks, CHUNK * events + 16, samples), jnp.int16)
     in_hbm = pl.BlockSpec(memory_space=pltpu.HBM)
     in_vmem = pl.BlockSpec(memory_space=pltpu.VMEM)
     dma = pltpu.SemaphoreType.DMA
@@ -325,7 +337,7 @@
             pltpu.VMEM((events, channels, samples), BF16),
             pltpu.VMEM((channels // 8, samples // 128, events * 8, 128), F32),
             pltpu.VMEM((channels, 3 * events, samples), BF16),
-            part, part, part, part, part,
+            part, code, code, code, code,
             pltpu.VMEM((3 * events, 3 * events), BF16),
             pltpu.VMEM((5, 16, 128), jnp.int32),
             pltpu.VMEM(forward.shape, BF16),

time: 50.5 us -> 49 us (0.970)
  Pallas kernels: 49 us -> 47.7 us
    pallas_call x1, Pallas kernels: 49 us -> 47.7 us  [local(): pl.pallas_call(kernel, out_shape=jax.ShapeDtypeStruct((events, channels,...]
where the time goes in v3:
time: 49 us; the launch traced here: 48.8 us
  Pallas kernels  47.7 us (97%)
  local copies, waits for them, and re-layouts  1.15 us (2%)
    pallas_call x1, Pallas kernels, local(): pl.pallas_call(kernel, out_shape=jax.ShapeDtypeStruct((events, channels,...  47.7 us
    unnamed x1, local copies, waits for them, and re-layouts  1.15 us

profile of v3, /device:TPU:1, one launch (start us, length us, event | category | flops | bytes accessed | tf_op | source)
XLA Modules:
  0.0 48.8 jit_solution(12621548193212409234)
XLA Ops:
  0.0 47.7 %event_correlation.1 = f32[64,24,256]{2,1,0:T(8,128)S(1)} custom-call(bf16[64,24,512]{2,1,0:T(8,128)(2,1)} %bitcast.6, s32[9,1,32]{2,1,0:T(1,128)} %bitcast.7, s32[9,1,32]{2,1,0:T(1,128)} %bitcast.8, s32[9,1,32]{2,1,0:T(1,128)} %bitcast.9, bf16[2,512,768]{2,1,0:T(8,128)(2,1)} %constant.4.clone.fwd_hbm, bf16[2,768,256]{2,1,0:T(8,128)(2,1)} %constant.5.clone.inv_hbm), custom_call_target="tpu_custom_call" | custom-call | flops 8000000000 | bytes 6000000 | tf_op jit(solution)/shard_map/event_correlation/pallas_call | solution.py:331
  47.7 1.1 %copy.8 = f32[1,1,64,24,256]{4,3,2,1,0:T(8,128)} copy(f32[1,1,64,24,256]{4,3,2,1,0:T(8,128)S(1)} %bitcast.5) | data formatting | bytes 3145728

commit v4 on v3

--- a/solution.py
+++ b/solution.py
@@ -16,6 +16,9 @@
 BINS = 128
 CHUNK = 2
 LAG = 2
+SETTLE = 5
+EARLY = 8
+AHEAD = 4
 CODE_MAX = 32767.0
 MESH = pl.DeviceIdType.MESH
 F32 = jnp.float32
@@ -58,11 +61,11 @@
 
 def kernel(
     traces, first, second, valid, fwd_hbm, inv_hbm, out,
-    raw, wide32, cells, part_own, sent_up, sent_down, got_up, got_down,
+    raw, wide32, cells, part_own, sent_low, sent_high, got_low, got_high,
     weights, codes, fwd, inv, held,
     load_sem, table_sem, code_send, code_recv,
-    x_send_left, x_send_right, x_from_left, x_from_right,
-    y_send_up, y_send_down, y_from_up, y_from_down,
+    x_send_low, x_send_high, x_from_low, x_from_high,
+    y_send_low, y_send_high, y_from_low, y_from_high,
 ):
     events, channels, samples = traces.shape
     lanes = samples // 128
@@ -95,23 +98,29 @@
         valid[:, 0, :] == 1, first[:, 0, :] * events + second[:, 0, :], -1
     )
 
-    def blank(has, slot, block, first_row, row_count):
+    def blank(has, slot, block, span, first_row, row_count):
         @pl.when(jnp.logical_not(has))
         def _():
             codes[slot] = jnp.full(codes.shape[1:], -1, jnp.int32)
 
             def clear(n, _):
                 block[n, first_row : first_row + row_count, :] = jnp.zeros(
-                    (row_count, samples), block.dtype
+                    (row_count, block.shape[2]), block.dtype
                 )
                 return 0
 
-            lax.fori_loop(0, block.shape[0], clear, 0)
-
-    blank(has_left, 1, cells, 0, events)
-    blank(has_right, 2, cells, 2 * events, events)
-    blank(has_up, 3, got_up, 0, got_up.shape[1])
-    blank(has_down, 4, got_down, 0, got_down.shape[1])
+            lax.fori_loop(*span, clear, 0)
+
+    split_at = EARLY * CHUNK
+    early, late = (0, EARLY), (EARLY, chunks)
+    blank(has_left, 1, cells, (0, split_at), 0, events)
+    blank(has_right, 2, cells, (0, split_at), 2 * events, events)
+    blank(has_up, 3, cells, (split_at, channels), 0, events)
+    blank(has_down, 4, cells, (split_at, channels), 2 * events, events)
+    blank(has_up, 3, got_low, early, 0, got_low.shape[1])
+    blank(has_down, 4, got_high, early, 0, got_high.shape[1])
+    blank(has_left, 1, got_low, late, 0, got_low.shape[1])
+    blank(has_right, 2, got_high, late, 0, got_high.shape[1])
 
     def turn(group):
         for i in range(lanes):
@@ -136,25 +145,56 @@
     ]
     has_from = {1: has_left, 2: has_right, 3: has_up, 4: has_down}
 
-    def x_left(k):
+    def traces_low(k, peer):
         block = pl.ds(k * CHUNK, CHUNK)
         return remote(
             cells.at[block, events : 2 * events, :], cells.at[block, 2 * events : 3 * events, :],
-            x_send_left.at[k], x_from_right.at[k], left,
-        )
-
-    def x_right(k):
+            x_send_low.at[k], x_from_high.at[k], peer,
+        )
+
+    def traces_high(k, peer):
         block = pl.ds(k * CHUNK, CHUNK)
         return remote(
             cells.at[block, events : 2 * events, :], cells.at[block, 0:events, :],
-            x_send_right.at[k], x_from_left.at[k], right,
-        )
-
-    def y_up(k):
-        return remote(sent_up.at[k], got_down.at[k], y_send_up.at[k], y_from_down.at[k], up)
-
-    def y_down(k):
-        return remote(sent_down.at[k], got_up.at[k], y_send_down.at[k], y_from_up.at[k], down)
+            x_send_high.at[k], x_from_low.at[k], peer,
+        )
+
+    def sums_low(k, peer):
+        return remote(sent_low.at[k], got_high.at[k], y_send_low.at[k], y_from_high.at[k], peer)
+
+    def sums_high(k, peer):
+        return remote(sent_high.at[k], got_low.at[k], y_send_high.at[k], y_from_low.at[k], peer)
+
+    across = ((has_left, left), (has_right, right))
+    along = ((has_up, up), (has_down, down))
+
+    def start(make_low, make_high, k, peers):
+        (has_low, low), (has_high, high) = peers
+        start_if(has_low, lambda: make_low(k, low))
+        start_if(has_high, lambda: make_high(k, high))
+
+    def wait_recv(make_low, make_high, k, peers):
+        (has_low, low), (has_high, high) = peers
+        wait_recv_if(has_low, lambda: make_high(k, high))
+        wait_recv_if(has_high, lambda: make_low(k, low))
+
+    def wait_send(make_low, make_high, k, peers):
+        (has_low, low), (has_high, high) = peers
+        wait_send_if(has_low, lambda: make_low(k, low))
+        wait_send_if(has_high, lambda: make_high(k, high))
+
+    def by_order(act, make_low, make_high, k, early_peers, late_peers):
+        if isinstance(k, int):
+            act(make_low, make_high, k, early_peers if k < EARLY else late_peers)
+            return
+
+        @pl.when(k < EARLY)
+        def _():
+            act(make_low, make_high, k, early_peers)
+
+        @pl.when(k >= EARLY)
+        def _():
+            act(make_low, make_high, k, late_peers)
 
     def start_if(has, make):
         @pl.when(has)
@@ -171,9 +211,8 @@
         def _():
             make().wait_recv()
 
-    def send_x(k):
-        start_if(has_left, lambda: x_left(k))
-        start_if(has_right, lambda: x_right(k))
+    def send_traces(k):
+        by_order(start, traces_low, traces_high, k, across, along)
 
     load.wait()
     turn(0)
@@ -181,10 +220,13 @@
     pl.semaphore_wait(barrier, peers)
     for copy, (has, _) in zip(code_copies, sides):
         start_if(has, lambda: copy)
-    for k in range(8 // CHUNK):
-        send_x(k)
-    for group in range(1, channels // 8):
+    for k in range(AHEAD):
+        send_traces(k)
+    for group in range(channels // 8 - 1, 0, -1):
         turn(group)
+        for k in range(group * 8 // CHUNK, (group + 1) * 8 // CHUNK):
+            if k >= EARLY:
+                send_traces(k)
 
     for copy, slot, (has, _) in zip(code_copies, (2, 1, 4, 3), sides):
         wait_send_if(has, lambda: copy)
@@ -207,17 +249,23 @@
             a, b, (((1,), (1,)), ((), ())), preferred_element_type=F32
         )
 
+    def count(target, target_heading, source, source_heading):
+        head, tail = ends(target, target_heading)
+        pairs = outer(head, tail)
+        head, tail = ends(source, source_heading)
+        return (pairs + outer(tail, head)).astype(BF16)
+
+    by_row = {-1: 3, 0: 0, 1: 4}
+    by_col = {-1: 1, 0: 0, 1: 2}
     for i in (-1, 0, 1):
-        target = {-1: 3, 0: 0, 1: 4}[i]
         for j in (-1, 0, 1):
-            source = {-1: 1, 0: 0, 1: 2}[j]
-            head, tail = ends(target, (1 - i) * 3 + (j + 1))
-            count = outer(head, tail)
-            head, tail = ends(source, (i + 1) * 3 + (1 - j))
-            count = count + outer(tail, head)
-            weights[
-                (i + 1) * events : (i + 2) * events, (j + 1) * events : (j + 2) * events
-            ] = count.astype(BF16)
+            rows_at = pl.ds((i + 1) * events, events)
+            weights[0, rows_at, (j + 1) * events : (j + 2) * events] = count(
+                by_row[i], (1 - i) * 3 + (j + 1), by_col[j], (i + 1) * 3 + (1 - j)
+            )
+            weights[1, rows_at, (j + 1) * events : (j + 2) * events] = count(
+                by_col[i], (j + 1) * 3 + (1 - i), by_row[j], (1 - j) * 3 + (i + 1)
+            )
 
     load_fwd.wait()
     load_inv.wait()
@@ -231,40 +279,36 @@
         peak = jnp.max(jnp.abs(part), axis=1, keepdims=True)
         power = jnp.ceil(jnp.log2(jnp.maximum(peak, 1e-30)) + 1e-4)
         code = jnp.round(part * (jnp.exp2(-power) * CODE_MAX))
-        ref[k, 0:size, :] = code.astype(jnp.int32).astype(jnp.int16)
+        code = code.astype(jnp.int32).astype(jnp.int16)
+        for i in range(lanes):
+            ref[k, i * size : (i + 1) * size, :] = code[:, i * 128 : (i + 1) * 128]
         band = jnp.sum(jnp.where(diagonal, power, 0.0), axis=0, keepdims=True)
-        ref[k, size : size + 16, 0:size] = (
+        ref[k, lanes * size : lanes * size + 16, 0:size] = (
             jnp.broadcast_to(band, (16, size)).astype(jnp.int32).astype(jnp.int16)
         )
 
     def decode(ref, k):
-        band = ref[k, size : size + 16, 0:size].astype(jnp.int32).astype(F32)[0:1]
+        band = ref[k, lanes * size : lanes * size + 16, 0:size].astype(jnp.int32).astype(F32)[0:1]
         power = jnp.sum(jnp.where(diagonal, band, 0.0), axis=1, keepdims=True)
-        code = ref[k, 0:size, :].astype(jnp.int32).astype(F32)
+        code = jnp.concatenate(
+            [ref[k, i * size : (i + 1) * size, :] for i in range(lanes)], axis=1
+        ).astype(jnp.int32).astype(F32)
         return code * (jnp.exp2(power) * (1.0 / CODE_MAX))
 
-    def gather(k):
-        @pl.when(k + 8 // CHUNK < chunks)
-        def _():
-            send_x(k + 8 // CHUNK)
-
-        wait_recv_if(has_left, lambda: x_right(k))
-        wait_recv_if(has_right, lambda: x_left(k))
-
-        parts = [dot(weights[...], cells[k * CHUNK + n]) for n in range(CHUNK)]
+    def gather(k, late):
+        wait_recv(traces_low, traces_high, k, along if late else across)
+        parts = [dot(weights[int(late)], cells[k * CHUNK + n]) for n in range(CHUNK)]
         for n in range(CHUNK):
             part_own[k * CHUNK + n] = parts[n][events : 2 * events]
-        encode(sent_up, k, jnp.concatenate([p[0:events] for p in parts], axis=0))
-        encode(sent_down, k, jnp.concatenate([p[2 * events :] for p in parts], axis=0))
-        start_if(has_up, lambda: y_up(k))
-        start_if(has_down, lambda: y_down(k))
+        encode(sent_low, k, jnp.concatenate([p[0:events] for p in parts], axis=0))
+        encode(sent_high, k, jnp.concatenate([p[2 * events :] for p in parts], axis=0))
+        start(sums_low, sums_high, k, across if late else along)
 
     def correlate(k):
-        wait_recv_if(has_up, lambda: y_down(k))
-        wait_recv_if(has_down, lambda: y_up(k))
+        by_order(wait_recv, sums_low, sums_high, k, along, across)
         block = pl.ds(k * CHUNK, CHUNK)
         x = cells[block, events : 2 * events, :].reshape(size, samples)
-        y = part_own[block].reshape(size, samples) + decode(got_up, k) + decode(got_down, k)
+        y = part_own[block].reshape(size, samples) + decode(got_low, k) + decode(got_high, k)
         y_high, y_low = split(y)
         stack3 = jnp.concatenate([x, y_high, y_low], axis=0)
         stack2 = jnp.concatenate([x, y_high], axis=0)
@@ -294,26 +338,37 @@
             for i in range(LAGS // 128):
                 out[:, place, i * 128 : (i + 1) * 128] = held[i].reshape(events, 8, 128)
 
+    def finish(k):
+        by_order(wait_send, traces_low, traces_high, k, across, along)
+        by_order(wait_send, sums_low, sums_high, k, along, across)
+
     def step(k, _):
-        @pl.when(k < chunks)
-        def _():
-            gather(k)
+        @pl.when(k + AHEAD < EARLY)
+        def _():
+            send_traces(k + AHEAD)
+
+        @pl.when(k < EARLY)
+        def _():
+            gather(k, False)
+
+        @pl.when((k >= EARLY - AHEAD) & (k < chunks - AHEAD))
+        def _():
+            gather(k + AHEAD, True)
 
         @pl.when(k >= LAG)
         def _():
             correlate(k - LAG)
 
+        @pl.when(k >= SETTLE)
+        def _():
+            finish(k - SETTLE)
+
         return 0
 
     lax.fori_loop(0, chunks + LAG, step, 0)
-    def finish(k, _):
-        wait_send_if(has_left, lambda: x_left(k))
-        wait_send_if(has_right, lambda: x_right(k))
-        wait_send_if(has_up, lambda: y_up(k))
-        wait_send_if(has_down, lambda: y_down(k))
-        return 0
-
-    lax.fori_loop(0, chunks, finish, 0)
+
+    for k in range(chunks + LAG - SETTLE, chunks):
+        finish(k)
 
 
 def by_heading(pairs):
@@ -324,7 +379,7 @@
     _, _, events, channels, samples = traces.shape
     chunks = channels // CHUNK
     part = pltpu.VMEM((channels, events, samples), F32)
-    code = pltpu.VMEM((chunks, CHUNK * events + 16, samples), jnp.int16)
+    code = pltpu.VMEM((chunks, CHUNK * events * samples // 128 + 16, 128), jnp.int16)
     in_hbm = pl.BlockSpec(memory_space=pltpu.HBM)
     in_vmem = pl.BlockSpec(memory_space=pltpu.VMEM)
     dma = pltpu.SemaphoreType.DMA
@@ -338,7 +393,7 @@
             pltpu.VMEM((channels // 8, samples // 128, events * 8, 128), F32),
             pltpu.VMEM((channels, 3 * events, samples), BF16),
             part, code, code, code, code,
-            pltpu.VMEM((3 * events, 3 * events), BF16),
+            pltpu.VMEM((2, 3 * events, 3 * events), BF16),
             pltpu.VMEM((5, 16, 128), jnp.int32),
             pltpu.VMEM(forward.shape, BF16),
             pltpu.VMEM(inverse.shape, BF16),

time: 49 us -> 43.9 us (0.90)
  Pallas kernels: 47.7 us -> 42.6 us
    pallas_call x1, Pallas kernels: 47.7 us -> 42.6 us  [local(): pl.pallas_call(kernel, out_shape=jax.ShapeDtypeStruct((events, channels,...]
where the time goes in v4:
time: 43.9 us; the launch traced here: 43.7 us
  Pallas kernels  42.6 us (97%)
  local copies, waits for them, and re-layouts  1.15 us (3%)
    pallas_call x1, Pallas kernels, local(): pl.pallas_call(kernel, out_shape=jax.ShapeDtypeStruct((events, channels,...  42.6 us
    unnamed x1, local copies, waits for them, and re-layouts  1.15 us

profile of v4, /device:TPU:1, one launch (start us, length us, event | category | flops | bytes accessed | tf_op | source)
XLA Modules:
  0.0 43.7 jit_solution(5271158418453738116)
XLA Ops:
  0.0 42.6 %event_correlation.1 = f32[64,24,256]{2,1,0:T(8,128)S(1)} custom-call(bf16[64,24,512]{2,1,0:T(8,128)(2,1)} %bitcast.6, s32[9,1,32]{2,1,0:T(1,128)} %bitcast.7, s32[9,1,32]{2,1,0:T(1,128)} %bitcast.8, s32[9,1,32]{2,1,0:T(1,128)} %bitcast.9, bf16[2,512,768]{2,1,0:T(8,128)(2,1)} %constant.4.clone.fwd_hbm, bf16[2,768,256]{2,1,0:T(8,128)(2,1)} %constant.5.clone.inv_hbm), custom_call_target="tpu_custom_call" | custom-call | flops 8000000000 | bytes 6000000 | tf_op jit(solution)/shard_map/event_correlation/pallas_call | solution.py:386
  42.6 1.1 %copy.8 = f32[1,1,64,24,256]{4,3,2,1,0:T(8,128)} copy(f32[1,1,64,24,256]{4,3,2,1,0:T(8,128)S(1)} %bitcast.5) | data formatting | bytes 3145728

commit v5 on v4

v5 whole, which is shorter than its diff:
```python
import functools
import math

import jax
import jax.numpy as jnp
import ml_dtypes
import numpy as np
from jax import lax
from jax.experimental import pallas as pl
from jax.experimental.pallas import tpu as pltpu
from jax.sharding import PartitionSpec as P

LAGS = 256
BLOCK = 128
SHIFTS = (-1, 0, 1)
CHUNK = 2
LAG = 3
SETTLE = 6
HYBRID = 5
EARLY = 8
AHEAD = 4
CODE_MAX = 32767.0
MESH = pl.DeviceIdType.MESH
F32 = jnp.float32
BF16 = jnp.bfloat16


def split_np(table):
    high = table.astype(ml_dtypes.bfloat16)
    low = (table - high.astype(np.float64)).astype(ml_dtypes.bfloat16)
    return np.stack([high, low])


def make_tables(samples):
    freq = np.arange(BLOCK, dtype=np.float64) + 0.5
    step = 2.0 * math.pi / (2 * BLOCK)
    phase = np.arange(BLOCK, dtype=np.float64)[:, None] * freq[None, :] * step
    forward = split_np(np.concatenate([np.cos(phase), -np.sin(phase)], axis=1))
    lag = np.arange(LAGS, dtype=np.float64) - LAGS // 2
    scale = 1.0 / (BLOCK * math.sqrt(samples))
    parts = []
    for d in SHIFTS:
        offset = lag - BLOCK * d
        phase = freq[:, None] * offset[None, :] * step
        inside = (np.abs(offset) < BLOCK)[None, :] * scale
        parts += [np.cos(phase) * inside, -np.sin(phase) * inside]
    return np.concatenate(list(forward), axis=0), split_np(np.concatenate(parts, axis=0))


def split(v):
    high = v.astype(BF16)
    return high, (v - high.astype(F32)).astype(BF16)


def dot(a, b):
    return jnp.dot(a, b, preferred_element_type=F32)


def when(condition):
    if isinstance(condition, bool):
        return (lambda body: body()) if condition else (lambda body: None)
    return pl.when(condition)


def kernel(
    traces, first, second, valid, fwd_hbm, inv_hbm, out,
    raw, wide32, cells, part_own, sent_low, sent_high, got_low, got_high,
    side, back_out, back_in, tail_out, tail_in, acc,
    weights, codes, fwd, inv, held,
    load_sem, table_sem, code_send, code_recv,
    x_send_low, x_send_high, x_from_low, x_from_high,
    y_send_low, y_send_high, y_from_low, y_from_high,
    side_send, side_recv, back_send, back_recv, tail_send, tail_recv,
):
    events, channels, samples = traces.shape
    lanes = samples // 128
    chunks = channels // CHUNK
    last = chunks - 1
    rows, cols = lax.axis_size("wide"), lax.axis_size("narrow")
    row, col = lax.axis_index("wide"), lax.axis_index("narrow")
    left = {"narrow": lax.rem(col + cols - 1, cols)}
    right = {"narrow": lax.rem(col + 1, cols)}
    up = {"wide": lax.rem(row + rows - 1, rows)}
    down = {"wide": lax.rem(row + 1, rows)}
    has_left, has_right = col > 0, col < cols - 1
    has_up, has_down = row > 0, row < rows - 1
    sides = ((has_left, left), (has_right, right), (has_up, up), (has_down, down))

    load = pltpu.make_async_copy(traces, raw, load_sem)
    load.start()
    barrier = pltpu.get_barrier_semaphore()
    for has, peer in sides:
        @pl.when(has)
        def _():
            pl.semaphore_signal(barrier, inc=1, device_id=peer, device_id_type=MESH)

    slots = first.shape[2]
    codes[0, 0:9, 0:slots] = jnp.where(
        valid[:, 0, :] == 1, first[:, 0, :] * events + second[:, 0, :], -1
    )

    def spread(group):
        for i in range(lanes):
            part = raw[:, group * 8 : (group + 1) * 8, i * 128 : (i + 1) * 128].astype(F32)
            wide32[group, i] = part.reshape(events * 8, 128)

    def turn(k):
        if k * CHUNK % 8 == 0:
            spread(k * CHUNK // 8)
        for c in range(k * CHUNK, (k + 1) * CHUNK):
            for i in range(lanes):
                lane_block = wide32[c // 8, i, pl.ds(c % 8, events, stride=8), :]
                cells[c, events : 2 * events, i * 128 : (i + 1) * 128] = lane_block.astype(BF16)

    back_rows = back_in.shape[1] // 2

    def remote(src, dst, send, recv, peer):
        return pltpu.make_async_remote_copy(
            src_ref=src, dst_ref=dst, send_sem=send, recv_sem=recv,
            device_id=peer, device_id_type=MESH,
        )

    code_copies = [
        remote(codes.at[0], codes.at[slot], code_send.at[slot - 1], code_recv.at[slot - 1], peer)
        for slot, peer in ((2, left), (1, right), (4, up), (3, down))
    ]
    has_from = {1: has_left, 2: has_right, 3: has_up, 4: has_down}

    def traces_low(k, peer):
        block = pl.ds(k * CHUNK, CHUNK)
        return remote(
            cells.at[block, events : 2 * events, :], cells.at[block, 2 * events : 3 * events, :],
            x_send_low.at[k], x_from_high.at[k], peer,
        )

    def traces_high(k, peer):
        block = pl.ds(k * CHUNK, CHUNK)
        return remote(
            cells.at[block, events : 2 * events, :], cells.at[block, 0:events, :],
            x_send_high.at[k], x_from_low.at[k], peer,
        )

    def sums_low(k, peer):
        return remote(sent_low.at[k], got_high.at[k], y_send_low.at[k], y_from_high.at[k], peer)

    def sums_high(k, peer):
        return remote(sent_high.at[k], got_low.at[k], y_send_high.at[k], y_from_low.at[k], peer)

    across = ((has_left, left), (has_right, right))
    along = ((has_up, up), (has_down, down))

    def start(make_low, make_high, k, peers):
        (has_low, low), (has_high, high) = peers
        start_if(has_low, lambda: make_low(k, low))
        start_if(has_high, lambda: make_high(k, high))

    def wait_recv(make_low, make_high, k, peers):
        (has_low, low), (has_high, high) = peers
        wait_recv_if(has_low, lambda: make_high(k, high))
        wait_recv_if(has_high, lambda: make_low(k, low))

    def wait_send(make_low, make_high, k, peers):
        (has_low, low), (has_high, high) = peers
        wait_send_if(has_low, lambda: make_low(k, low))
        wait_send_if(has_high, lambda: make_high(k, high))

    def by_axis(act, make_low, make_high, k, is_across):
        @when(is_across)
        def _():
            act(make_low, make_high, k, across)

        @when(not is_across if isinstance(is_across, bool) else jnp.logical_not(is_across))
        def _():
            act(make_low, make_high, k, along)

    def on_traces(act, k):
        by_axis(act, traces_low, traces_high, k, (k >= HYBRID) & (k < EARLY))

    def on_sums(act, k):
        by_axis(act, sums_low, sums_high, k, k >= EARLY)

    def side_copy(k, n):
        return remote(
            cells.at[k * CHUNK + n, events : 2 * events, :],
            side.at[k, n * events : (n + 1) * events, :],
            side_send.at[k, n], side_recv.at[k, n], (right, left)[n],
        )

    def back_copy(k, n):
        span = slice(n * back_rows, (n + 1) * back_rows)
        return remote(
            back_out.at[k, span, :], back_in.at[k, span, :],
            back_send.at[k, n], back_recv.at[k, n], (left, right)[n],
        )

    has_target, has_origin = (has_right, has_left), (has_left, has_right)

    def start_if(has, make):
        @pl.when(has)
        def _():
            make().start()

    def wait_send_if(has, make):
        @pl.when(has)
        def _():
            make().wait_send()

    def wait_recv_if(has, make):
        @pl.when(has)
        def _():
            make().wait_recv()

    load.wait()
    load_fwd = pltpu.make_async_copy(fwd_hbm, fwd, table_sem.at[0])
    load_inv = pltpu.make_async_copy(inv_hbm, inv, table_sem.at[1])
    load_fwd.start()
    load_inv.start()

    turn(0)
    peers = sum(has.astype(jnp.int32) for has, _ in sides)
    pl.semaphore_wait(barrier, peers)
    for k in range(HYBRID):
        if k > 0:
            turn(k)
        for n in range(CHUNK):
            start_if(has_target[n], lambda: side_copy(k, n))
        if k == 0:
            for copy, (has, _) in zip(code_copies, sides):
                start_if(has, lambda: copy)
        on_traces(start, k)
    for k in range(HYBRID, chunks):
        turn(k)

    def blank(has, slot, block, span, first_row, row_count):
        @pl.when(jnp.logical_not(has))
        def _():
            codes[slot] = jnp.full(codes.shape[1:], -1, jnp.int32)

            def clear(n, _):
                block[n, first_row : first_row + row_count, :] = jnp.zeros(
                    (row_count, block.shape[2]), block.dtype
                )
                return 0

            lax.fori_loop(*span, clear, 0)

    hybrid_to, early_to = HYBRID * CHUNK, EARLY * CHUNK
    for span in ((0, hybrid_to), (early_to, channels)):
        blank(has_up, 3, cells, span, 0, events)
        blank(has_down, 4, cells, span, 2 * events, events)
    blank(has_left, 1, cells, (hybrid_to, early_to), 0, events)
    blank(has_right, 2, cells, (hybrid_to, early_to), 2 * events, events)
    blank(has_up, 3, got_low, (0, EARLY), 0, got_low.shape[1])
    blank(has_down, 4, got_high, (0, EARLY), 0, got_high.shape[1])
    blank(has_left, 1, got_low, (EARLY, last), 0, got_low.shape[1])
    blank(has_right, 2, got_high, (EARLY, last), 0, got_high.shape[1])
    blank(has_left, 1, tail_in.at[0], (0, CHUNK), 0, tail_in.shape[2])
    blank(has_right, 2, tail_in.at[1], (0, CHUNK), 0, tail_in.shape[2])
    blank(has_left, 1, side, (0, HYBRID), 0, events)
    blank(has_right, 2, side, (0, HYBRID), events, events)
    blank(has_right, 2, back_in, (0, HYBRID), 0, back_rows)
    blank(has_left, 1, back_in, (0, HYBRID), back_rows, back_rows)

    for copy, slot, (has, _) in zip(code_copies, (2, 1, 4, 3), sides):
        wait_send_if(has, lambda: copy)
        wait_recv_if(has_from[slot], lambda: copy)

    ids = lax.broadcasted_iota(jnp.int32, (events, slots), 0)

    def ends(slot, heading):
        code = codes[slot, heading : heading + 1, 0:slots]
        live = code >= 0
        head = jnp.where(live, code // events, -1)
        tail = jnp.where(live, code % events, -1)
        return (
            jnp.where(ids == head, 1.0, 0.0).astype(BF16),
            jnp.where(ids == tail, 1.0, 0.0).astype(BF16),
        )

    def outer(a, b):
        return lax.dot_general(
            a, b, (((1,), (1,)), ((), ())), preferred_element_type=F32
        )

    def count(target, target_heading, source, source_heading):
        head, tail = ends(target, target_heading)
        pairs = outer(head, tail)
        head, tail = ends(source, source_heading)
        return (pairs + outer(tail, head)).astype(BF16)

    by_row = {-1: 3, 0: 0, 1: 4}
    by_col = {-1: 1, 0: 0, 1: 2}
    for i in (-1, 0, 1):
        for j in (-1, 0, 1):
            rows_at = pl.ds((i + 1) * events, events)
            weights[0, rows_at, (j + 1) * events : (j + 2) * events] = count(
                by_row[i], (1 - i) * 3 + (j + 1), by_col[j], (i + 1) * 3 + (1 - j)
            )
            weights[1, rows_at, (j + 1) * events : (j + 2) * events] = count(
                by_col[i], (j + 1) * 3 + (1 - i), by_row[j], (1 - j) * 3 + (i + 1)
            )

    load_fwd.wait()
    load_inv.wait()

    size = CHUNK * events

    def diagonal(n):
        at = [lax.broadcasted_iota(jnp.int32, (n, n), dim) for dim in (0, 1)]
        return at[0] == at[1]

    def encoded(part):
        n = part.shape[0]
        peak = jnp.max(jnp.abs(part), axis=1, keepdims=True)
        power = jnp.ceil(jnp.log2(jnp.maximum(peak, 1e-30)) + 1e-4)
        code = jnp.round(part * (jnp.exp2(-power) * CODE_MAX))
        band = jnp.sum(jnp.where(diagonal(n), power, 0.0), axis=0, keepdims=True)
        band = jnp.broadcast_to(band, (16, n)).astype(jnp.int32).astype(jnp.int16)
        return code.astype(jnp.int32).astype(jnp.int16), band

    def encode(ref, at, part):
        n = part.shape[0]
        code, band = encoded(part)
        for i in range(lanes):
            ref[*at, i * n : (i + 1) * n, :] = code[:, i * 128 : (i + 1) * 128]
        ref[*at, lanes * n : lanes * n + 16, 0:n] = band

    def decode(ref, at, n):
        band = ref[*at, lanes * n : lanes * n + 16, 0:n].astype(jnp.int32).astype(F32)[0:1]
        power = jnp.sum(jnp.where(diagonal(n), band, 0.0), axis=1, keepdims=True)
        code = jnp.concatenate(
            [ref[*at, i * n : (i + 1) * n, :] for i in range(lanes)], axis=1
        ).astype(jnp.int32).astype(F32)
        return code * (jnp.exp2(power) * (1.0 / CODE_MAX))

    def gather(k, late):
        wait_recv(traces_low, traces_high, k, along if late else across)
        parts = [dot(weights[int(late)], cells[k * CHUNK + n]) for n in range(CHUNK)]
        for n in range(CHUNK):
            part_own[k * CHUNK + n] = parts[n][events : 2 * events]
        encode(sent_low, (k,), jnp.concatenate([p[0:events] for p in parts], axis=0))
        encode(sent_high, (k,), jnp.concatenate([p[2 * events :] for p in parts], axis=0))
        start(sums_low, sums_high, k, across if late else along)

    def correlation(x, y):
        size = x.shape[0]
        y_high, y_low = split(y)
        stack = []
        for v in (x, y_high, y_low):
            for i in range(lanes):
                block = v[:, i * BLOCK : (i + 1) * BLOCK]
                stack.append(jnp.concatenate([block, block], axis=1))
        spectra = dot(jnp.concatenate(stack, axis=0), fwd[...])
        spectra = [spectra[n * size : (n + 1) * size] for n in range(3 * lanes)]
        xs = spectra[:lanes]
        ys = [spectra[lanes + i] + spectra[2 * lanes + i] for i in range(lanes)]
        total = jnp.zeros((size, LAGS), F32)
        for n, d in enumerate(SHIFTS):
            real, imag = 0.0, 0.0
            for i in range(max(0, -d), min(lanes, lanes - d)):
                xr, xi = xs[i][:, :BLOCK], xs[i][:, BLOCK:]
                yr, yi = ys[i + d][:, :BLOCK], ys[i + d][:, BLOCK:]
                real = real + (xr * yr + xi * yi)
                imag = imag + (xr * yi - xi * yr)
            s_high, s_low = split(jnp.concatenate([real, imag], axis=1))
            span = slice(n * 2 * BLOCK, (n + 1) * 2 * BLOCK)
            both = dot(jnp.concatenate([s_high, s_low], axis=0), inv[0, span, :])
            total = total + (both[:size] + both[size:] + dot(s_high, inv[1, span, :]))
        return total

    def hybrid_gather(k):
        on_traces(wait_recv, k)
        for n in range(CHUNK):
            wait_recv_if(has_origin[n], lambda: side_copy(k, n))
        c = k * CHUNK
        column_first = dot(weights[1, 0 : 2 * events, :], cells[c])
        column_second = dot(weights[1, events : 3 * events, :], cells[c + 1])
        side_first = dot(weights[0, :, 0:events], side[k, 0:events, :])
        side_second = dot(weights[0, :, 2 * events : 3 * events], side[k, events : 2 * events, :])
        part_own[c] = column_first[events:] + side_first[events : 2 * events]
        part_own[c + 1] = column_second[0:events] + side_second[events : 2 * events]
        encode(sent_low, (k,), jnp.concatenate([side_first[0:events], side_second[0:events]], axis=0))
        encode(
            sent_high, (k,),
            jnp.concatenate([side_first[2 * events :], side_second[2 * events :]], axis=0),
        )
        on_sums(start, k)
        returned = jnp.concatenate([column_first[0:events], column_second[events:]], axis=0)
        code, band = encoded(correlation(side[k], returned))
        for n in range(CHUNK):
            base = n * back_rows
            for i in range(LAGS // 128):
                back_out[k, base + i * events : base + (i + 1) * events, :] = code[
                    n * events : (n + 1) * events, i * 128 : (i + 1) * 128
                ]
            back_out[k, base + back_rows - 16 : base + back_rows, :] = band
            start_if(has_origin[n], lambda: back_copy(k, n))

    def add_back(k):
        for n in range(CHUNK):
            wait_recv_if(has_target[n], lambda: back_copy(k, n))
        bands = [
            back_in[k, (n + 1) * back_rows - 16 : (n + 1) * back_rows, :].astype(jnp.int32)
            for n in range(CHUNK)
        ]
        lane = lax.broadcasted_iota(jnp.int32, (16, size), 1)
        band = jnp.where(lane < events, bands[0], bands[1]).astype(F32)[0:1]
        power = jnp.sum(jnp.where(diagonal(size), band, 0.0), axis=1, keepdims=True)
        code = jnp.concatenate(
            [
                jnp.concatenate(
                    [
                        back_in[k, n * back_rows + i * events : n * back_rows + (i + 1) * events, :]
                        for i in range(LAGS // 128)
                    ],
                    axis=1,
                )
                for n in range(CHUNK)
            ],
            axis=0,
        )
        acc[...] += code.astype(jnp.int32).astype(F32) * (jnp.exp2(power) * (1.0 / CODE_MAX))

    def tail_low(n):
        return remote(
            tail_out.at[0, n], tail_in.at[1, n], tail_send.at[0, n], tail_recv.at[1, n], left
        )

    def tail_high(n):
        return remote(
            tail_out.at[1, n], tail_in.at[0, n], tail_send.at[1, n], tail_recv.at[0, n], right
        )

    def gather_last():
        wait_recv(traces_low, traces_high, last, along)
        for n in range(CHUNK):
            c = last * CHUNK + n
            part = dot(weights[1], cells[c])
            part_own[c] = part[events : 2 * events]
            encode(tail_out, (0, n), part[0:events])
            encode(tail_out, (1, n), part[2 * events :])
            start_if(has_left, lambda: tail_low(n))
            start_if(has_right, lambda: tail_high(n))

    def correlate_last():
        for n in range(CHUNK):
            c = last * CHUNK + n
            wait_recv_if(has_left, lambda: tail_high(n))
            wait_recv_if(has_right, lambda: tail_low(n))
            y = part_own[c] + decode(tail_in, (0, n), events) + decode(tail_in, (1, n), events)
            keep(c, correlation(cells[c, events : 2 * events, :], y))

    def keep(c, rows):
        for i in range(LAGS // 128):
            held[i, pl.ds(c % 8, events, stride=8), :] = rows[:, i * 128 : (i + 1) * 128]

    def flush(group):
        place = pl.ds(group * 8, 8)
        if not isinstance(group, int):
            place = pl.ds(pl.multiple_of(group * 8, 8), 8)
        for i in range(LAGS // 128):
            out[:, place, i * 128 : (i + 1) * 128] = held[i].reshape(events, 8, 128)

    def correlate(k):
        on_sums(wait_recv, k)
        block = pl.ds(k * CHUNK, CHUNK)
        x = cells[block, events : 2 * events, :].reshape(size, samples)
        y = part_own[block].reshape(size, samples) + decode(got_low, (k,), size) + decode(got_high, (k,), size)
        acc[...] = correlation(x, y)

        @pl.when(k < HYBRID)
        def _():
            add_back(k)

        total = acc[...]
        per_group = 8 // CHUNK
        for n in range(CHUNK):
            keep(k * CHUNK + n, total[n * events : (n + 1) * events])

        @pl.when(k % per_group == per_group - 1)
        def _():
            flush(k // per_group)

    def finish(k):
        on_traces(wait_send, k)

        @when(k < last)
        def _():
            on_sums(wait_send, k)

        @when(k < HYBRID)
        def _():
            for n in range(CHUNK):
                wait_send_if(has_target[n], lambda: side_copy(k, n))
                wait_send_if(has_origin[n], lambda: back_copy(k, n))

    def step(k, _):
        ahead = k + AHEAD

        @pl.when((ahead >= max(AHEAD, HYBRID)) & (ahead < EARLY))
        def _():
            start(traces_low, traces_high, ahead, across)

        @pl.when(k < chunks - EARLY)
        def _():
            start(traces_low, traces_high, k + EARLY, along)

        @pl.when(k < HYBRID)
        def _():
            hybrid_gather(k)

        @pl.when((k >= HYBRID) & (k < EARLY))
        def _():
            gather(k, False)

        @pl.when((ahead >= EARLY) & (ahead < last))
        def _():
            gather(ahead, True)

        @pl.when(ahead == last)
        def _():
            gather_last()

        @pl.when((k >= LAG) & (k < last + LAG))
        def _():
            correlate(k - LAG)

        @pl.when(k >= SETTLE)
        def _():
            finish(k - SETTLE)

        return 0

    lax.fori_loop(0, last + LAG, step, 0)
    for k in range(last + LAG - SETTLE, chunks):
        finish(k)
    correlate_last()
    flush(channels // 8 - 1)
    for n in range(CHUNK):
        wait_send_if(has_left, lambda: tail_low(n))
        wait_send_if(has_right, lambda: tail_high(n))


def by_heading(pairs):
    return pairs.transpose(0, 2, 1, 3)[0]


def local(forward, inverse, traces, pair_first, pair_second, pair_valid):
    _, _, events, channels, samples = traces.shape
    chunks = channels // CHUNK
    part = pltpu.VMEM((channels, events, samples), F32)
    code = pltpu.VMEM((chunks, CHUNK * events * samples // 128 + 16, 128), jnp.int16)
    back = pltpu.VMEM((HYBRID, CHUNK * (events * LAGS // 128 + 16), 128), jnp.int16)
    tail = pltpu.VMEM((2, CHUNK, events * samples // 128 + 16, 128), jnp.int16)
    in_hbm = pl.BlockSpec(memory_space=pltpu.HBM)
    in_vmem = pl.BlockSpec(memory_space=pltpu.VMEM)
    dma = pltpu.SemaphoreType.DMA
    out = pl.pallas_call(
        kernel,
        out_shape=jax.ShapeDtypeStruct((events, channels, LAGS), F32),
        in_specs=[in_hbm, in_vmem, in_vmem, in_vmem, in_hbm, in_hbm],
        out_specs=in_vmem,
        scratch_shapes=[
            pltpu.VMEM((events, channels, samples), BF16),
            pltpu.VMEM((channels // 8, samples // 128, events * 8, 128), F32),
            pltpu.VMEM((channels, 3 * events, samples), BF16),
            part, code, code, code, code,
            pltpu.VMEM((HYBRID, CHUNK * events, samples), BF16),
            back, back, tail, tail,
            pltpu.VMEM((CHUNK * events, LAGS), F32),
            pltpu.VMEM((2, 3 * events, 3 * events), BF16),
            pltpu.VMEM((5, 16, 128), jnp.int32),
            pltpu.VMEM(forward.shape, BF16),
            pltpu.VMEM(inverse.shape, BF16),
            pltpu.VMEM((LAGS // 128, events * 8, 128), F32),
            dma, dma((2,)), dma((4,)), dma((4,)),
        ] + [dma((chunks,))] * 8 + [dma((HYBRID, CHUNK))] * 4 + [dma((2, CHUNK))] * 2,
        compiler_params=pltpu.CompilerParams(
            collective_id=0, has_side_effects=True, vmem_limit_bytes=40 * 1024 * 1024
        ),
        cost_estimate=pl.CostEstimate(
            flops=8 * 10**9, bytes_accessed=6 * 10**6, transcendentals=0
        ),
        name="event_correlation",
    )(*[pltpu.with_memory_space_constraint(v, pltpu.HBM) for v in (traces[0, 0], by_heading(pair_first), by_heading(pair_second), by_heading(pair_valid), forward, inverse)])
    return out[None, None]


def solution(mesh):
    forward, inverse = make_tables(512)
    spec4 = P("wide", "narrow", None, None)
    spec5 = P("wide", "narrow", None, None, None)

    def run(traces, pair_first, pair_second, pair_valid):
        return local(
            jnp.asarray(forward), jnp.asarray(inverse), traces, pair_first, pair_second, pair_valid
        )

    return jax.shard_map(
        run, mesh=mesh, in_specs=(spec5, spec4, spec4, spec4), out_specs=spec5, check_vma=False
    )
```

time: 43.9 us -> 40.8 us (0.929)
  Pallas kernels: 42.6 us -> 39.3 us
    pallas_call x1, Pallas kernels: 42.6 us -> 39.3 us  [local(): pl.pallas_call(kernel, out_shape=jax.ShapeDtypeStruct((events, channels,...]
where the time goes in v5:
time: 40.8 us; the launch traced here: 40.5 us
  Pallas kernels  39.3 us (96%)
  local copies, waits for them, and re-layouts  1.15 us (3%)
    pallas_call x1, Pallas kernels, local(): pl.pallas_call(kernel, out_shape=jax.ShapeDtypeStruct((events, channels,...  39.3 us
    unnamed x1, local copies, waits for them, and re-layouts  1.15 us

profile of v5, /device:TPU:1, one launch (start us, length us, event | category | flops | bytes accessed | tf_op | source)
XLA Modules:
  0.0 40.5 jit_solution(7508837102566053139)
XLA Ops:
  0.0 39.3 %event_correlation.1 = f32[64,24,256]{2,1,0:T(8,128)S(1)} custom-call(bf16[64,24,512]{2,1,0:T(8,128)(2,1)} %bitcast.6, s32[9,1,32]{2,1,0:T(1,128)} %bitcast.7, s32[9,1,32]{2,1,0:T(1,128)} %bitcast.8, s32[9,1,32]{2,1,0:T(1,128)} %bitcast.9, bf16[256,256]{1,0:T(8,128)(2,1)} %constant.4.clone.fwd_hbm, bf16[2,768,256]{2,1,0:T(8,128)(2,1)} %constant.5.clone.inv_hbm), custom_call_target="tpu_custom_call" | custom-call | flops 8000000000 | bytes 6000000 | tf_op jit(solution)/shard_map/event_correlation/pallas_call | solution.py:558
  39.3 1.1 %copy.8 = f32[1,1,64,24,256]{4,3,2,1,0:T(8,128)} copy(f32[1,1,64,24,256]{4,3,2,1,0:T(8,128)S(1)} %bitcast.5) | data formatting | bytes 3145728

commit v6 on v5

--- a/solution.py
+++ b/solution.py
@@ -14,8 +14,9 @@
 BLOCK = 128
 SHIFTS = (-1, 0, 1)
 CHUNK = 2
-LAG = 3
-SETTLE = 6
+LAG = 5
+SETTLE = 8
+FORWARD = 1
 HYBRID = 5
 EARLY = 8
 AHEAD = 4
@@ -112,7 +113,7 @@
                 lane_block = wide32[c // 8, i, pl.ds(c % 8, events, stride=8), :]
                 cells[c, events : 2 * events, i * 128 : (i + 1) * 128] = lane_block.astype(BF16)
 
-    back_rows = back_in.shape[1] // 2
+    back_rows = events * LAGS // 128
 
     def remote(src, dst, send, recv, peer):
         return pltpu.make_async_remote_copy(
@@ -186,12 +187,23 @@
             side_send.at[k, n], side_recv.at[k, n], (right, left)[n],
         )
 
-    def back_copy(k, n):
-        span = slice(n * back_rows, (n + 1) * back_rows)
+    def back_copy(pair, n, rows):
         return remote(
-            back_out.at[k, span, :], back_in.at[k, span, :],
-            back_send.at[k, n], back_recv.at[k, n], (left, right)[n],
-        )
+            back_out.at[pair, n, 0:rows, :], back_in.at[pair, n, 0:rows, :],
+            back_send.at[pair, n], back_recv.at[pair, n], (left, right)[n],
+        )
+
+    def on_back(act, has, k, place):
+        @when((k % 2 == place) & (k < HYBRID // 2 * 2))
+        def _():
+            for n in range(CHUNK):
+                act(has[n], lambda: back_copy(k // 2, n, 2 * back_rows + 16))
+
+        if HYBRID % 2:
+            @when(k == HYBRID - 1)
+            def _():
+                for n in range(CHUNK):
+                    act(has[n], lambda: back_copy(k // 2, n, back_rows + 16))
 
     has_target, has_origin = (has_right, has_left), (has_left, has_right)
 
@@ -230,6 +242,8 @@
         on_traces(start, k)
     for k in range(HYBRID, chunks):
         turn(k)
+    for k in range(EARLY, chunks):
+        start(traces_low, traces_high, k, along)
 
     def blank(has, slot, block, span, first_row, row_count):
         @pl.when(jnp.logical_not(has))
@@ -258,8 +272,9 @@
     blank(has_right, 2, tail_in.at[1], (0, CHUNK), 0, tail_in.shape[2])
     blank(has_left, 1, side, (0, HYBRID), 0, events)
     blank(has_right, 2, side, (0, HYBRID), events, events)
-    blank(has_right, 2, back_in, (0, HYBRID), 0, back_rows)
-    blank(has_left, 1, back_in, (0, HYBRID), back_rows, back_rows)
+    for pair in range(back_in.shape[0]):
+        blank(has_right, 2, back_in.at[pair], (0, 1), 0, back_in.shape[2])
+        blank(has_left, 1, back_in.at[pair], (1, 2), 0, back_in.shape[2])
 
     for copy, slot, (has, _) in zip(code_copies, (2, 1, 4, 3), sides):
         wait_send_if(has, lambda: copy)
@@ -387,30 +402,39 @@
         on_sums(start, k)
         returned = jnp.concatenate([column_first[0:events], column_second[events:]], axis=0)
         code, band = encoded(correlation(side[k], returned))
-        for n in range(CHUNK):
-            base = n * back_rows
+        pair, half = k // 2, k % 2
+        sublane = lax.broadcasted_iota(jnp.int32, (16, size), 0)
+        for n in range(CHUNK):
             for i in range(LAGS // 128):
-                back_out[k, base + i * events : base + (i + 1) * events, :] = code[
+                at = pl.multiple_of(16 + half * back_rows + i * events, 16)
+                back_out[pair, n, pl.ds(at, events), :] = code[
                     n * events : (n + 1) * events, i * 128 : (i + 1) * 128
                 ]
-            back_out[k, base + back_rows - 16 : base + back_rows, :] = band
-            start_if(has_origin[n], lambda: back_copy(k, n))
+            before = back_out[pair, n, 0:16, :].astype(jnp.int32)
+            back_out[pair, n, 0:16, :] = jnp.where(
+                sublane >= 8 * half, band.astype(jnp.int32), before
+            ).astype(jnp.int16)
+        on_back(start_if, has_origin, k, 1)
 
     def add_back(k):
-        for n in range(CHUNK):
-            wait_recv_if(has_target[n], lambda: back_copy(k, n))
-        bands = [
-            back_in[k, (n + 1) * back_rows - 16 : (n + 1) * back_rows, :].astype(jnp.int32)
-            for n in range(CHUNK)
-        ]
+        on_back(wait_recv_if, has_target, k, 0)
+        pair, half = k // 2, k % 2
+        bands = [back_in[pair, n, 0:16, :].astype(jnp.int32).astype(F32) for n in range(CHUNK)]
         lane = lax.broadcasted_iota(jnp.int32, (16, size), 1)
-        band = jnp.where(lane < events, bands[0], bands[1]).astype(F32)[0:1]
+        band = jnp.where(lane < events, bands[0], bands[1])
+        band = jnp.where(half == 0, band[0:1], band[8:9])
         power = jnp.sum(jnp.where(diagonal(size), band, 0.0), axis=1, keepdims=True)
         code = jnp.concatenate(
             [
                 jnp.concatenate(
                     [
-                        back_in[k, n * back_rows + i * events : n * back_rows + (i + 1) * events, :]
+                        back_in[
+                            pair, n,
+                            pl.ds(
+                                pl.multiple_of(16 + half * back_rows + i * events, 16), events
+                            ),
+                            :,
+                        ]
                         for i in range(LAGS // 128)
                     ],
                     axis=1,
@@ -421,45 +445,65 @@
         )
         acc[...] += code.astype(jnp.int32).astype(F32) * (jnp.exp2(power) * (1.0 / CODE_MAX))
 
+    def tail_rows(n):
+        return pl.ds(0, lanes * events + (16 if n == 0 else 0))
+
     def tail_low(n):
         return remote(
-            tail_out.at[0, n], tail_in.at[1, n], tail_send.at[0, n], tail_recv.at[1, n], left
+            tail_out.at[0, n, tail_rows(n)], tail_in.at[1, n, tail_rows(n)],
+            tail_send.at[0, n], tail_recv.at[1, n], left,
         )
 
     def tail_high(n):
         return remote(
-            tail_out.at[1, n], tail_in.at[0, n], tail_send.at[1, n], tail_recv.at[0, n], right
+            tail_out.at[1, n, tail_rows(n)], tail_in.at[0, n, tail_rows(n)],
+            tail_send.at[1, n], tail_recv.at[0, n], right,
         )
 
     def gather_last():
         wait_recv(traces_low, traces_high, last, along)
-        for n in range(CHUNK):
-            c = last * CHUNK + n
-            part = dot(weights[1], cells[c])
-            part_own[c] = part[events : 2 * events]
-            encode(tail_out, (0, n), part[0:events])
-            encode(tail_out, (1, n), part[2 * events :])
+        parts = [dot(weights[1], cells[last * CHUNK + n]) for n in range(CHUNK)]
+        for n in range(CHUNK):
+            part_own[last * CHUNK + n] = parts[n][events : 2 * events]
+        for way, first_row in ((0, 0), (1, 2 * events)):
+            code, band = encoded(
+                jnp.concatenate([p[first_row : first_row + events] for p in parts], axis=0)
+            )
+            for n in range(CHUNK):
+                for i in range(lanes):
+                    tail_out[way, n, i * events : (i + 1) * events, :] = code[
+                        n * events : (n + 1) * events, i * 128 : (i + 1) * 128
+                    ]
+            tail_out[way, 0, lanes * events : lanes * events + 16, :] = band
+        for n in range(CHUNK):
             start_if(has_left, lambda: tail_low(n))
             start_if(has_right, lambda: tail_high(n))
+
+    def tail_part(way, n):
+        band = tail_in[way, 0, lanes * events : lanes * events + 16, :]
+        band = band.astype(jnp.int32).astype(F32)[0:1]
+        power = jnp.sum(jnp.where(diagonal(size), band, 0.0), axis=1, keepdims=True)
+        code = jnp.concatenate(
+            [tail_in[way, n, i * events : (i + 1) * events, :] for i in range(lanes)], axis=1
+        ).astype(jnp.int32).astype(F32)
+        return code * (jnp.exp2(power[n * events : (n + 1) * events]) * (1.0 / CODE_MAX))
 
     def correlate_last():
         for n in range(CHUNK):
             c = last * CHUNK + n
             wait_recv_if(has_left, lambda: tail_high(n))
             wait_recv_if(has_right, lambda: tail_low(n))
-            y = part_own[c] + decode(tail_in, (0, n), events) + decode(tail_in, (1, n), events)
+            y = part_own[c] + tail_part(0, n) + tail_part(1, n)
             keep(c, correlation(cells[c, events : 2 * events, :], y))
 
     def keep(c, rows):
         for i in range(LAGS // 128):
-            held[i, pl.ds(c % 8, events, stride=8), :] = rows[:, i * 128 : (i + 1) * 128]
+            held[c // 8, i, pl.ds(c % 8, events, stride=8), :] = rows[:, i * 128 : (i + 1) * 128]
 
     def flush(group):
         place = pl.ds(group * 8, 8)
-        if not isinstance(group, int):
-            place = pl.ds(pl.multiple_of(group * 8, 8), 8)
         for i in range(LAGS // 128):
-            out[:, place, i * 128 : (i + 1) * 128] = held[i].reshape(events, 8, 128)
+            out[:, place, i * 128 : (i + 1) * 128] = held[group, i].reshape(events, 8, 128)
 
     def correlate(k):
         on_sums(wait_recv, k)
@@ -473,13 +517,8 @@
             add_back(k)
 
         total = acc[...]
-        per_group = 8 // CHUNK
         for n in range(CHUNK):
             keep(k * CHUNK + n, total[n * events : (n + 1) * events])
-
-        @pl.when(k % per_group == per_group - 1)
-        def _():
-            flush(k // per_group)
 
     def finish(k):
         on_traces(wait_send, k)
@@ -492,7 +531,7 @@
         def _():
             for n in range(CHUNK):
                 wait_send_if(has_target[n], lambda: side_copy(k, n))
-                wait_send_if(has_origin[n], lambda: back_copy(k, n))
+            on_back(wait_send_if, has_origin, k, 1)
 
     def step(k, _):
         ahead = k + AHEAD
@@ -501,10 +540,6 @@
         def _():
             start(traces_low, traces_high, ahead, across)
 
-        @pl.when(k < chunks - EARLY)
-        def _():
-            start(traces_low, traces_high, k + EARLY, along)
-
         @pl.when(k < HYBRID)
         def _():
             hybrid_gather(k)
@@ -521,9 +556,22 @@
         def _():
             gather_last()
 
-        @pl.when((k >= LAG) & (k < last + LAG))
-        def _():
-            correlate(k - LAG)
+        place = k - LAG
+        moved = (place >= HYBRID) & (place < HYBRID + FORWARD)
+        held_back = (place >= HYBRID + FORWARD) & (place < EARLY + FORWARD)
+
+        @pl.when((place >= 0) & (place < last))
+        def _():
+            correlate(
+                place
+                + (EARLY - HYBRID) * moved.astype(jnp.int32)
+                - FORWARD * held_back.astype(jnp.int32)
+            )
+
+        @pl.when(place == last - 1)
+        def _():
+            for group in range(channels // 8 - 1):
+                flush(group)
 
         @pl.when(k >= SETTLE)
         def _():
@@ -550,7 +598,8 @@
     chunks = channels // CHUNK
     part = pltpu.VMEM((channels, events, samples), F32)
     code = pltpu.VMEM((chunks, CHUNK * events * samples // 128 + 16, 128), jnp.int16)
-    back = pltpu.VMEM((HYBRID, CHUNK * (events * LAGS // 128 + 16), 128), jnp.int16)
+    pairs = -(-HYBRID // 2)
+    back = pltpu.VMEM((pairs, CHUNK, 2 * events * LAGS // 128 + 16, 128), jnp.int16)
     tail = pltpu.VMEM((2, CHUNK, events * samples // 128 + 16, 128), jnp.int16)
     in_hbm = pl.BlockSpec(memory_space=pltpu.HBM)
     in_vmem = pl.BlockSpec(memory_space=pltpu.VMEM)
@@ -572,9 +621,9 @@
             pltpu.VMEM((5, 16, 128), jnp.int32),
             pltpu.VMEM(forward.shape, BF16),
             pltpu.VMEM(inverse.shape, BF16),
-            pltpu.VMEM((LAGS // 128, events * 8, 128), F32),
+            pltpu.VMEM((channels // 8, LAGS // 128, events * 8, 128), F32),
             dma, dma((2,)), dma((4,)), dma((4,)),
-        ] + [dma((chunks,))] * 8 + [dma((HYBRID, CHUNK))] * 4 + [dma((2, CHUNK))] * 2,
+        ] + [dma((chunks,))] * 8 + [dma((HYBRID, CHUNK))] * 2 + [dma((pairs, CHUNK))] * 2 + [dma((2, CHUNK))] * 2,
         compiler_params=pltpu.CompilerParams(
             collective_id=0, has_side_effects=True, vmem_limit_bytes=40 * 1024 * 1024
         ),

time: 40.8 us -> 40.3 us (0.988)
  no operation moved by 1% of the time
where the time goes in v6:
time: 40.3 us; the launch traced here: 40.2 us
  Pallas kernels  39 us (97%)
  local copies, waits for them, and re-layouts  1.15 us (3%)
    pallas_call x1, Pallas kernels, local(): pl.pallas_call(kernel, out_shape=jax.ShapeDtypeStruct((events, channels,...  39 us
    unnamed x1, local copies, waits for them, and re-layouts  1.15 us

profile of v6, /device:TPU:1, one launch (start us, length us, event | category | flops | bytes accessed | tf_op | source)
XLA Modules:
  0.0 40.2 jit_solution(6097967938942862556)
XLA Ops:
  0.0 39.0 %event_correlation.1 = f32[64,24,256]{2,1,0:T(8,128)S(1)} custom-call(bf16[64,24,512]{2,1,0:T(8,128)(2,1)} %bitcast.6, s32[9,1,32]{2,1,0:T(1,128)} %bitcast.7, s32[9,1,32]{2,1,0:T(1,128)} %bitcast.8, s32[9,1,32]{2,1,0:T(1,128)} %bitcast.9, bf16[256,256]{1,0:T(8,128)(2,1)} %constant.4.clone.fwd_hbm, bf16[2,768,256]{2,1,0:T(8,128)(2,1)} %constant.5.clone.inv_hbm), custom_call_target="tpu_custom_call" | custom-call | flops 8000000000 | bytes 6000000 | tf_op jit(solution)/shard_map/event_correlation/pallas_call | solution.py:607
  39.0 1.1 %copy.8 = f32[1,1,64,24,256]{4,3,2,1,0:T(8,128)} copy(f32[1,1,64,24,256]{4,3,2,1,0:T(8,128)S(1)} %bitcast.5) | data formatting | bytes 3145728

commit v7 on v6

--- a/solution.py
+++ b/solution.py
@@ -17,6 +17,7 @@
 LAG = 5
 SETTLE = 8
 FORWARD = 1
+LOADS = 4
 HYBRID = 5
 EARLY = 8
 AHEAD = 4
@@ -87,8 +88,16 @@
     has_up, has_down = row > 0, row < rows - 1
     sides = ((has_left, left), (has_right, right), (has_up, up), (has_down, down))
 
-    load = pltpu.make_async_copy(traces, raw, load_sem)
-    load.start()
+    share = events // LOADS
+    loads = [
+        pltpu.make_async_copy(
+            traces.at[i * share : (i + 1) * share], raw.at[i * share : (i + 1) * share],
+            load_sem.at[i],
+        )
+        for i in range(LOADS)
+    ]
+    for load in loads:
+        load.start()
     barrier = pltpu.get_barrier_semaphore()
     for has, peer in sides:
         @pl.when(has)
@@ -222,7 +231,8 @@
         def _():
             make().wait_recv()
 
-    load.wait()
+    for load in loads:
+        load.wait()
     load_fwd = pltpu.make_async_copy(fwd_hbm, fwd, table_sem.at[0])
     load_inv = pltpu.make_async_copy(inv_hbm, inv, table_sem.at[1])
     load_fwd.start()
@@ -244,6 +254,7 @@
         turn(k)
     for k in range(EARLY, chunks):
         start(traces_low, traces_high, k, along)
+    start(traces_low, traces_high, HYBRID, across)
 
     def blank(has, slot, block, span, first_row, row_count):
         @pl.when(jnp.logical_not(has))
@@ -536,9 +547,9 @@
     def step(k, _):
         ahead = k + AHEAD
 
-        @pl.when((ahead >= max(AHEAD, HYBRID)) & (ahead < EARLY))
-        def _():
-            start(traces_low, traces_high, ahead, across)
+        @pl.when((k >= 2) & (k < EARLY - HYBRID - 1 + 2))
+        def _():
+            start(traces_low, traces_high, k + HYBRID + 1 - 2, across)
 
         @pl.when(k < HYBRID)
         def _():
@@ -622,7 +633,7 @@
             pltpu.VMEM(forward.shape, BF16),
             pltpu.VMEM(inverse.shape, BF16),
             pltpu.VMEM((channels // 8, LAGS // 128, events * 8, 128), F32),
-            dma, dma((2,)), dma((4,)), dma((4,)),
+            dma((LOADS,)), dma((2,)), dma((4,)), dma((4,)),
         ] + [dma((chunks,))] * 8 + [dma((HYBRID, CHUNK))] * 2 + [dma((pairs, CHUNK))] * 2 + [dma((2, CHUNK))] * 2,
         compiler_params=pltpu.CompilerParams(
             collective_id=0, has_side_effects=True, vmem_limit_bytes=40 * 1024 * 1024

time: 40.3 us -> 40.4 us (level)
  no operation moved by 1% of the time
where the time goes in v7:
time: 40.4 us; the launch traced here: 40.2 us
  Pallas kernels  39.1 us (97%)
  local copies, waits for them, and re-layouts  1.15 us (3%)
    pallas_call x1, Pallas kernels, local(): pl.pallas_call(kernel, out_shape=jax.ShapeDtypeStruct((events, channels,...  39.1 us
    unnamed x1, local copies, waits for them, and re-layouts  1.15 us

profile of v7, /device:TPU:1, one launch (start us, length us, event | category | flops | bytes accessed | tf_op | source)
XLA Modules:
  0.0 40.2 jit_solution(8359747789028254913)
XLA Ops:
  0.0 39.1 %event_correlation.1 = f32[64,24,256]{2,1,0:T(8,128)S(1)} custom-call(bf16[64,24,512]{2,1,0:T(8,128)(2,1)} %bitcast.6, s32[9,1,32]{2,1,0:T(1,128)} %bitcast.7, s32[9,1,32]{2,1,0:T(1,128)} %bitcast.8, s32[9,1,32]{2,1,0:T(1,128)} %bitcast.9, bf16[256,256]{1,0:T(8,128)(2,1)} %constant.4.clone.fwd_hbm, bf16[2,768,256]{2,1,0:T(8,128)(2,1)} %constant.5.clone.inv_hbm), custom_call_target="tpu_custom_call" | custom-call | flops 8000000000 | bytes 6000000 | tf_op jit(solution)/shard_map/event_correlation/pallas_call | solution.py:618
  39.1 1.1 %copy.8 = f32[1,1,64,24,256]{4,3,2,1,0:T(8,128)} copy(f32[1,1,64,24,256]{4,3,2,1,0:T(8,128)S(1)} %bitcast.5) | data formatting | bytes 3145728

commit v8 on v7

--- a/solution.py
+++ b/solution.py
@@ -183,8 +183,32 @@
         def _():
             act(make_low, make_high, k, along)
 
+    def two_low(k, peer):
+        block = pl.ds(k * CHUNK, 2 * CHUNK)
+        return remote(
+            cells.at[block, events : 2 * events, :], cells.at[block, 2 * events : 3 * events, :],
+            x_send_low.at[k], x_from_high.at[k], peer,
+        )
+
+    def two_high(k, peer):
+        block = pl.ds(k * CHUNK, 2 * CHUNK)
+        return remote(
+            cells.at[block, events : 2 * events, :], cells.at[block, 0:events, :],
+            x_send_high.at[k], x_from_low.at[k], peer,
+        )
+
     def on_traces(act, k):
-        by_axis(act, traces_low, traces_high, k, (k >= HYBRID) & (k < EARLY))
+        @when((k >= HYBRID) & (k < EARLY - 2))
+        def _():
+            act(traces_low, traces_high, k, across)
+
+        @when(k == EARLY - 2)
+        def _():
+            act(two_low, two_high, k, across)
+
+        @when((k < HYBRID) | (k >= EARLY))
+        def _():
+            act(traces_low, traces_high, k, along)
 
     def on_sums(act, k):
         by_axis(act, sums_low, sums_high, k, k >= EARLY)
@@ -360,7 +384,7 @@
         return code * (jnp.exp2(power) * (1.0 / CODE_MAX))
 
     def gather(k, late):
-        wait_recv(traces_low, traces_high, k, along if late else across)
+        on_traces(wait_recv, k)
         parts = [dot(weights[int(late)], cells[k * CHUNK + n]) for n in range(CHUNK)]
         for n in range(CHUNK):
             part_own[k * CHUNK + n] = parts[n][events : 2 * events]
@@ -547,9 +571,9 @@
     def step(k, _):
         ahead = k + AHEAD
 
-        @pl.when((k >= 2) & (k < EARLY - HYBRID - 1 + 2))
-        def _():
-            start(traces_low, traces_high, k + HYBRID + 1 - 2, across)
+        @pl.when(k == 2)
+        def _():
+            start(two_low, two_high, EARLY - 2, across)
 
         @pl.when(k < HYBRID)
         def _():

time: 40.4 us -> 41.5 us (1.027)
  the two profiles are of different devices: /device:TPU:1 before, /device:TPU:26 now
where the time goes in v8:
time: 41.5 us; the launch traced here: 41.4 us
  Pallas kernels  40.2 us (97%)
  local copies, waits for them, and re-layouts  1.15 us (3%)
    pallas_call x1, Pallas kernels, local(): pl.pallas_call(kernel, out_shape=jax.ShapeDtypeStruct((events, channels,...  40.2 us
    unnamed x1, local copies, waits for them, and re-layouts  1.15 us

profile of v8, /device:TPU:26, one launch (start us, length us, event | category | flops | bytes accessed | tf_op | source)
XLA Modules:
  0.0 41.4 jit_solution(10145962442369346323)
XLA Ops:
  0.0 40.2 %event_correlation.1 = f32[64,24,256]{2,1,0:T(8,128)S(1)} custom-call(bf16[64,24,512]{2,1,0:T(8,128)(2,1)} %bitcast.6, s32[9,1,32]{2,1,0:T(1,128)} %bitcast.7, s32[9,1,32]{2,1,0:T(1,128)} %bitcast.8, s32[9,1,32]{2,1,0:T(1,128)} %bitcast.9, bf16[256,256]{1,0:T(8,128)(2,1)} %constant.4.clone.fwd_hbm, bf16[2,768,256]{2,1,0:T(8,128)(2,1)} %constant.5.clone.inv_hbm), custom_call_target="tpu_custom_call" | custom-call | flops 8000000000 | bytes 6000000 | tf_op jit(solution)/shard_map/event_correlation/pallas_call | solution.py:642
  40.2 1.1 %copy.8 = f32[1,1,64,24,256]{4,3,2,1,0:T(8,128)} copy(f32[1,1,64,24,256]{4,3,2,1,0:T(8,128)S(1)} %bitcast.5) | data formatting | bytes 3145728
